TPU v7x, 1024 devices: a whole 8x8x8 slice. The times are simulated.
1024 devices in a mesh: dp: 8 (over x), fsdp: 128 (over z, y, core).
Axes of the slice: x: 8, y: 8, z: 8, core: 2. Of those that a mesh axis runs over, the one named last changes fastest.
Arguments:
- acts: bfloat16 [16384, 8192], P('fsdp', 'dp'), may hold values from -6 to 6
- out_grad: bfloat16 [16384, 28672], P(None, 'fsdp'), may hold values from -0.09375 to 0.09375
- basis: bfloat16 [8192, 512], P('dp'), may hold values from -0.0625 to 0.0625
- first_moment: float32 [512, 28672], P('dp', 'fsdp'), may hold values from -6 to 6
- second_moment: float32 [512, 28672], P('dp', 'fsdp'), may hold values from 0.01 to 1
Outputs:
- update: float32 [8192, 28672], P('dp', 'fsdp')
- new_first: float32 [512, 28672], P('dp', 'fsdp')
- new_second: float32 [512, 28672], P('dp', 'fsdp')
All inputs are finite; a program needn't handle non-finite values.
Results may differ from a plain program's by a relative error of at most 0.0029.
Values may be sent and summed in bfloat16 or wider, within the bound.
No kernel may reach another device: no remote copies, remote signals or barrier semaphores. Data moves between devices by JAX's collectives and lax.ppermute only.
A program may use at most 128 MiB of HBM per device.

v0:
```python
import jax
import jax.numpy as jnp
from jax import lax
from jax.sharding import PartitionSpec as P

STEP = 1000


beta_first = 0.9
beta_second = 0.999
adam_epsilon = 1e-08


def moments_step(grad_low, first_moment, second_moment):
    new_first = beta_first * first_moment + (1.0 - beta_first) * grad_low
    new_second = beta_second * second_moment + (1.0 - beta_second) * grad_low * grad_low
    corrected_first = new_first / (1.0 - beta_first**STEP)
    corrected_second = new_second / (1.0 - beta_second**STEP)
    direction = (corrected_first / (jnp.sqrt(corrected_second) + adam_epsilon)).astype(jnp.bfloat16)
    return (new_first, new_second, direction)


def per_device(acts, out_grad, basis, first_moment, second_moment):
    local_terms = jnp.dot(acts, basis, preferred_element_type=jnp.float32)
    hidden_cols = out_grad.shape[1]
    share = lax.psum_scatter(local_terms, "dp", scatter_dimension=1, tiled=True)
    token_rows = out_grad.astype(jnp.float32)
    grad_rows = lax.dot_general(
        lax.all_gather(share, "fsdp", axis=0, tiled=True),
        token_rows,
        (((0,), (0,)), ((), ())),
        precision=lax.Precision.HIGHEST,
        preferred_element_type=jnp.float32,
    )
    new_first, new_second, direction = moments_step(grad_rows, first_moment, second_moment)
    zero_update = jnp.zeros((basis.shape[0], hidden_cols), jnp.float32)
    piece = lax.all_gather(direction, "dp", axis=0, tiled=True)
    basis_cols = lax.slice_in_dim(basis, 0, piece.shape[0], axis=1)
    update = zero_update + jnp.dot(basis_cols, piece, preferred_element_type=jnp.float32)
    return (update, new_first, new_second)


def solution(mesh):
    return jax.shard_map(
        per_device,
        mesh=mesh,
        in_specs=(
            P("fsdp", "dp"),
            P(None, "fsdp"),
            P("dp", None),
            P("dp", "fsdp"),
            P("dp", "fsdp"),
        ),
        out_specs=(P("dp", "fsdp"), P("dp", "fsdp"), P("dp", "fsdp")),
        check_vma=False,
    )
```

profile of v0, /device:TPU:4, one launch (start us, length us, event | category | flops | bytes accessed | tf_op | source)
XLA Modules:
  0.0 212.9 jit_solution(15414834691361745066)
XLA Ops:
  7.2 0.0 copy-start
  7.2 0.0 reduce-scatter.4.cloned.1.call-start
  7.2 1.2 copy-done
  8.4 2.2 %convolution_bitcast_fusion.1 = f32[512,128]{1,0:T(8,128)} fusion(bf16[128,1024]{1,0:T(8,128)(2,1)} %param.5, bf16[1024,512]{1,0:T(8,128)(2,1)S(1)} %copy-done), kind=kOutput, calls=%fused_computation.1 | convolution fusion | flops 134217728 | bytes 1572864
  10.6 0.0 reduce-scatter.4.cloned.1.call-update
  10.6 0.0 all-gather.2.cloned.1.call-start
  10.6 52.9 %reduce-scatter.4.cloned.1.call-done = f32[64,128]{1,0:T(8,128)} async-done(((f32[512,128]{1,0:T(8,128)}), f32[64,128]{1,0:T(8,128)}) %reduce-scatter.4.cloned.1.call-update) | async-done | bytes 32784
  63.6 1.5 copy.9
  65.1 0.0 all-gather.2.cloned.1.call-update
  65.1 100.7 %all-gather.2.cloned.1.call-done = f32[16384,64]{1,0:T(8,128)} async-done(((f32[128,64]{1,0:T(8,128)}), f32[16384,64]{1,0:T(8,128)}) %all-gather.2.cloned.1.call-update) | async-done | bytes 4194320 | tf_op jit(solution)/shard_map/all_gather | solution.py:29
  165.8 13.2 %divide_convert_fusion = (bf16[64,224]{1,0:T(8,128)(2,1)S(1)}, f32[64,224]{1,0:T(8,128)}, f32[64,224]{1,0:T(8,128)}) fusion(f32[64,224]{1,0:T(8,128)} %param.9, f32[64,224]{1,0:T(8,128)} %param.8, f32[16384,64]{1,0:T(8,128)} %all-gather.2.cloned.1.call-done, bf16[16384,224]{0,1:T(8,128)(2,1)} %param.6), kind=kOutput, calls=%fused_computation.4 | convolution fusion | flops 2818729984 | bytes 11792384 | tf_op jit(solution)/shard_map/dot_general | solution.py:28
  179.0 25.7 %all_gather.7 = bf16[512,224]{1,0:T(8,128)(2,1)S(1)} all-gather(bf16[64,224]{1,0:T(8,128)(2,1)S(1)} %get-tuple-element.3), channel_id=1, replica_groups=mesh['dp'=8,'fsdp'=128] {'dp'}, dimensions={0}, use_global_device_ids=true | all-gather | bytes 258048 | tf_op jit(solution)/shard_map/all_gather | solution.py:37
  204.7 1.4 convolution_bitcast_fusion
Async XLA Ops:
  7.2 1.2 copy-start
  7.2 56.4 %reduce-scatter.4.cloned.1.call-start = ((), (), s32[]{:S(2)}) async-start(), calls=%async_computation.2 | async-start | bytes 294912
  10.6 155.2 %all-gather.2.cloned.1.call-start = ((), (), s32[]{:S(2)}) async-start(), calls=%async_computation.1 | async-start | bytes 8454144 | tf_op jit(solution)/shard_map/all_gather | solution.py:29
Sparse Core Ops, SparseCore 0:
  12.0 51.5 reduce-scatter.3
  69.2 96.5 all-gather.1
where the time goes:
time: 213 us
  waiting for transfers between devices  154 us (72%)
  blocking collectives  25.7 us (12%)
  matrix products  16.8 us (8%)
  between operations  14 us (7%)
  local copies, waits for them, and re-layouts  2.66 us (1%)
    all_gather x1, waiting for transfers between devices, per_device(): lax.all_gather(share, 'fsdp', axis=0, tiled=True)  101 us
    unnamed x3, waiting for transfers between devices  53 us
    all_gather x1, blocking collectives, per_device(): piece = lax.all_gather(direction, 'dp', axis=0, tiled=True)  25.7 us
    dot_general x1, matrix products, per_device(): lax.dot_general(lax.all_gather(share, 'fsdp', axis=0, tiled=True), token_...  13.2 us
  transfers between devices with their start and end apart: 2, of which 2 were waited for; matrix products, arithmetic and copies ran while one was open for 0% of the time, Pallas kernels for 0%

commit v1 on v0

v1 whole, which is shorter than its diff:
```python
import functools

import jax
import jax.numpy as jnp
import numpy as np
from jax import lax
from jax.experimental import pallas as pl
from jax.experimental.pallas import tpu as pltpu
from jax.sharding import Mesh
from jax.sharding import PartitionSpec as P

STEP = 1000


beta_first = 0.9
beta_second = 0.999
adam_epsilon = 1e-08


def moments_step(grad_low, first_moment, second_moment):
    new_first = beta_first * first_moment + (1.0 - beta_first) * grad_low
    new_second = beta_second * second_moment + (1.0 - beta_second) * grad_low * grad_low
    corrected_first = new_first / (1.0 - beta_first**STEP)
    corrected_second = new_second / (1.0 - beta_second**STEP)
    direction = (corrected_first / (jnp.sqrt(corrected_second) + adam_epsilon)).astype(jnp.bfloat16)
    return (new_first, new_second, direction)


def grad_kernel(steps, core_ref, own_ref, other_ref, grad_t_ref, first_ref, second_ref,
                new_first_ref, new_second_ref, spread_ref, total_ref):
    step = pl.program_id(0)

    @pl.when(step == 0)
    def _():
        total_ref[...] = jnp.zeros_like(total_ref)

    is_first = core_ref[0] == 0
    chips = own_ref.shape[0]
    pieces = []
    for chip in range(chips):
        own, other = own_ref[chip], other_ref[chip]
        pieces += [jnp.where(is_first, own, other), jnp.where(is_first, other, own)]
    projected = jnp.concatenate(pieces, axis=1)
    total_ref[...] += lax.dot_general(
        projected, grad_t_ref[...], (((1,), (1,)), ((), ())), preferred_element_type=jnp.float32
    )

    @pl.when(step == steps - 1)
    def _():
        new_first, new_second, direction = moments_step(total_ref[...], first_ref[...], second_ref[...])
        new_first_ref[...] = new_first
        new_second_ref[...] = new_second
        for copy in range(spread_ref.shape[0]):
            spread_ref[copy] = direction


def grad_and_moments(core, own, other, grad_t, first_moment, second_moment, copies):
    chips, rank, rows = own.shape
    hidden, tokens = grad_t.shape
    steps = 8
    whole = lambda shape: pl.BlockSpec(shape, lambda s, c: (0,) * len(shape))
    return pl.pallas_call(
        functools.partial(grad_kernel, steps),
        grid_spec=pltpu.PrefetchScalarGridSpec(
            num_scalar_prefetch=1,
            grid=(steps,),
            in_specs=[
                pl.BlockSpec((chips // steps, rank, rows), lambda s, c: (s, 0, 0)),
                pl.BlockSpec((chips // steps, rank, rows), lambda s, c: (s, 0, 0)),
                pl.BlockSpec((hidden, tokens // steps), lambda s, c: (0, s)),
                whole((rank, hidden)),
                whole((rank, hidden)),
            ],
            out_specs=[whole((rank, hidden)), whole((rank, hidden)), whole((copies, rank, hidden))],
            scratch_shapes=[pltpu.VMEM((rank, hidden), jnp.float32)],
        ),
        out_shape=[
            jax.ShapeDtypeStruct((rank, hidden), jnp.float32),
            jax.ShapeDtypeStruct((rank, hidden), jnp.float32),
            jax.ShapeDtypeStruct((copies, rank, hidden), jnp.bfloat16),
        ],
        compiler_params=pltpu.CompilerParams(vmem_limit_bytes=32 * 1024 * 1024),
        cost_estimate=pl.CostEstimate(
            flops=2 * rank * hidden * tokens,
            bytes_accessed=2 * (hidden * tokens + rank * tokens),
            transcendentals=rank * hidden,
        ),
    )(core, own, other, grad_t, first_moment, second_moment)


def per_device(acts, out_grad, basis, first_moment, second_moment):
    splits = lax.axis_size("x")
    chips = lax.axis_size("z") * lax.axis_size("y")
    tokens = acts.shape[0]
    rank = basis.shape[1] // splits
    local_terms = lax.dot_general(
        basis, acts, (((0,), (1,)), ((), ())), preferred_element_type=jnp.float32
    ).astype(jnp.bfloat16)
    terms = lax.all_to_all(
        local_terms.reshape(splits, rank, tokens), "x", split_axis=0, concat_axis=0, tiled=True
    )
    share = jnp.sum(terms.astype(jnp.float32), axis=0).astype(jnp.bfloat16)
    spread = jnp.broadcast_to(share[None], (chips, rank, tokens))
    own = lax.all_to_all(spread, ("z", "y"), split_axis=0, concat_axis=0, tiled=True)
    other = lax.ppermute(own, "c", [(0, 1), (1, 0)])
    core = lax.axis_index("c").astype(jnp.int32).reshape(1)
    new_first, new_second, direction = grad_and_moments(
        core, own, other, out_grad.T, first_moment, second_moment, splits
    )
    pieces = lax.all_to_all(direction, "x", split_axis=0, concat_axis=0, tiled=True)
    piece = pieces.reshape(splits * rank, pieces.shape[2])
    update = jnp.dot(basis, piece, preferred_element_type=jnp.float32)
    return (update, new_first, new_second)


def solution(mesh):
    chips = Mesh(np.asarray(mesh.devices).reshape(8, 8, 8, 2), ("x", "z", "y", "c"))
    fsdp = ("z", "y", "c")
    return jax.shard_map(
        per_device,
        mesh=chips,
        in_specs=(P(fsdp, "x"), P(None, fsdp), P("x", None), P("x", fsdp), P("x", fsdp)),
        out_specs=(P("x", fsdp), P("x", fsdp), P("x", fsdp)),
        check_vma=False,
    )
```

time: 213 us -> 101 us (0.47)
  the two profiles are of different devices: /device:TPU:4 before, /device:TPU:1 now
where the time goes in v1:
time: 101 us
  blocking collectives  77.8 us (77%)
  starting transfers between devices  6.61 us (7%)
  local copies, waits for them, and re-layouts  6.23 us (6%)
  Pallas kernels  4.58 us (5%)
  matrix products  2.87 us (3%)
  waiting for transfers between devices  2.26 us (2%)
    all_to_all x1, blocking collectives, per_device(): lax.all_to_all(spread, ('z', 'y'), split_axis=0, concat_axis=0, tiled=True)  48.5 us
    all_to_all x1, blocking collectives, per_device(): lax.all_to_all(local_terms.reshape(splits, rank, tokens), 'x', split_axis...  15 us
    all_to_all x1, blocking collectives, per_device(): lax.all_to_all(direction, 'x', split_axis=0, concat_axis=0, tiled=True)  14.2 us
    ppermute x1, starting transfers between devices, per_device(): other = lax.ppermute(own, 'c', [(0, 1), (1, 0)])  6.61 us
    unnamed x8, local copies, waits for them, and re-layouts  5.98 us
    pallas_call x1, Pallas kernels, grad_and_moments(): pl.pallas_call(functools.partial(grad_kernel, steps), grid_spec=pltpu.Pre...  4.58 us
    ppermute x1, waiting for transfers between devices, per_device(): other = lax.ppermute(own, 'c', [(0, 1), (1, 0)])  2.26 us
  transfers between devices with their start and end apart: 1, of which 1 were waited for; matrix products, arithmetic and copies ran while one was open for 0% of the time, Pallas kernels for 0%

profile of v1, /device:TPU:1, one launch (start us, length us, event | category | flops | bytes accessed | tf_op | source)
XLA Modules:
  0.0 101.0 jit_solution(17163449251962580313)
XLA Ops:
  0.6 0.0 copy-start
  0.6 1.2 %copy-done = bf16[1024,512]{1,0:T(8,128)(2,1)S(1)} copy-done((bf16[1024,512]{1,0:T(8,128)(2,1)S(1)}, bf16[1024,512]{1,0:T(8,128)(2,1)}, u32[]{:S(2)}) %copy-start) | copy-done | bytes 1048600
  1.9 1.4 %convolution_convert_fusion = bf16[512,128]{1,0:T(8,128)(2,1)S(1)} fusion(bf16[1024,512]{1,0:T(8,128)(2,1)S(1)} %copy-done, bf16[128,1024]{1,0:T(8,128)(2,1)} %param.5), kind=kOutput, calls=%fused_computation.1 | convolution fusion | flops 134283264 | bytes 1441792 | tf_op jit(solution)/shard_map/dot_general | solution.py:96
  3.3 15.0 %all_to_all.15 = bf16[8,64,128]{2,1,0:T(8,128)(2,1)S(1)} all-to-all(bf16[8,64,128]{2,1,0:T(8,128)(2,1)S(1)} %bitcast.12), channel_id=1, replica_groups=mesh['x'=8,'z'=8,'y'=8,'c'=2] {'x'}, dimensions={0} | all-to-all | bytes 262144 | tf_op jit(solution)/shard_map/all_to_all | solution.py:99
  18.4 0.2 broadcast_in_dim.2
  18.6 48.5 %all_to_all.16.own_ref = bf16[64,64,128]{2,1,0:T(8,128)(2,1)S(1)} all-to-all(bf16[64,64,128]{2,1,0:T(8,128)(2,1)S(1)} %broadcast_in_dim.2), channel_id=1, replica_groups=mesh['x'=8,'z'=8,'y'=8,'c'=2] {'z','y'}, dimensions={0} | all-to-all | bytes 2097152 | tf_op jit(solution)/shard_map/all_to_all | solution.py:104
  67.2 6.6 %collective-permute-start = (bf16[64,64,128]{2,1,0:T(8,128)(2,1)S(1)}, bf16[64,64,128]{2,1,0:T(8,128)(2,1)S(1)}, u32[]{:S(2)}, u32[]{:S(2)}) collective-permute-start(bf16[64,64,128]{2,1,0:T(8,128)(2,1)S(1)} %all_to_all.16.own_ref), channel_id=1, source_target_pairs={{0,1},{1,0},{2,3},{3,2},{4,5},{5,4},{6,7},{7,6},{8,9},{9,8},{10,11... | collective-permute-start | bytes 3145736 | tf_op jit(solution)/shard_map/ppermute | solution.py:105
  73.8 2.3 %collective-permute-done.other_ref = bf16[64,64,128]{2,1,0:T(8,128)(2,1)S(1)} collective-permute-done((bf16[64,64,128]{2,1,0:T(8,128)(2,1)S(1)}, bf16[64,64,128]{2,1,0:T(8,128)(2,1)S(1)}, u32[]{:S(2)}, u32[]{:S(2)}) %collective-permute-start) | collective-permute-done | bytes 1048608 | tf_op jit(solution)/shard_map/ppermute | solution.py:105
  76.0 0.0 copy-start.1
  76.0 3.1 %copy-done.1 = bf16[16384,224]{0,1:T(8,128)(2,1)S(1)} copy-done((bf16[16384,224]{0,1:T(8,128)(2,1)S(1)}, bf16[16384,224]{0,1:T(8,128)(2,1)}, u32[]{:S(2)}) %copy-start.1) | copy-done | bytes 7340056
  79.1 0.0 copy-start.2
  79.1 0.8 copy-done.2
  80.0 0.0 copy-start.3
  80.0 0.8 copy-done.3
  80.8 4.6 %shard_map.76 = (f32[64,224]{1,0:T(8,128)}, f32[64,224]{1,0:T(8,128)}, bf16[8,64,224]{2,1,0:T(8,128)(2,1)S(1)}) custom-call(s32[1]{0:T(128)} %bitcast.core_ref, bf16[64,64,128]{2,1,0:T(8,128)(2,1)S(1)} %all_to_all.16.own_ref, bf16[64,64,128]{2,1,0:T(8,128)(2,1)S(1)} %collective-permute-done.other_ref, bf16[224,16384]{1,0:T(8,128)(2,1)S(1)} %bitcast.10, ...), custom_call_target="tpu_custom_call" | custom-call | flops 469762048 | bytes 9437184 | tf_op jit(solution)/shard_map/pallas_call | solution.py:62
  85.4 14.2 %all_to_all.17 = bf16[8,64,224]{2,1,0:T(8,128)(2,1)S(1)} all-to-all(bf16[8,64,224]{2,1,0:T(8,128)(2,1)S(1)} %get-tuple-element.6), channel_id=1, replica_groups=mesh['x'=8,'z'=8,'y'=8,'c'=2] {'x'}, dimensions={0} | all-to-all | bytes 458752 | tf_op jit(solution)/shard_map/all_to_all | solution.py:110
  99.6 1.4 %convolution_bitcast_fusion = f32[1024,224]{0,1:T(8,128)} fusion(bf16[512,224]{1,0:T(8,128)(2,1)S(1)} %bitcast.11, bf16[1024,512]{1,0:T(8,128)(2,1)S(1)} %copy-done), kind=kOutput, calls=%fused_computation | convolution fusion | flops 234881024 | bytes 2195456 | tf_op jit(solution)/shard_map/dot_general | solution.py:112
  (1 shorter events, 0.0 us)
Async XLA Ops:
  0.6 1.2 %copy-start = (bf16[1024,512]{1,0:T(8,128)(2,1)S(1)}, bf16[1024,512]{1,0:T(8,128)(2,1)}, u32[]{:S(2)}) copy-start(bf16[1024,512]{1,0:T(8,128)(2,1)} %param.7) | copy-start | bytes 3145732
  67.2 8.9 %collective-permute-start = (bf16[64,64,128]{2,1,0:T(8,128)(2,1)S(1)}, bf16[64,64,128]{2,1,0:T(8,128)(2,1)S(1)}, u32[]{:S(2)}, u32[]{:S(2)}) collective-permute-start(bf16[64,64,128]{2,1,0:T(8,128)(2,1)S(1)} %all_to_all.16.own_ref), channel_id=1, source_target_pairs={{0,1},{1,0},{2,3},{3,2},{4,5},{5,4},{6,7},{7,6},{8,9},{9,8},{10,11... | collective-permute-start | bytes 3145736 | tf_op jit(solution)/shard_map/ppermute | solution.py:105
  76.0 3.1 %copy-start.1 = (bf16[16384,224]{0,1:T(8,128)(2,1)S(1)}, bf16[16384,224]{0,1:T(8,128)(2,1)}, u32[]{:S(2)}) copy-start(bf16[16384,224]{0,1:T(8,128)(2,1)} %param.6) | copy-start | bytes 22020100
  79.1 0.8 copy-start.2
  80.0 0.8 copy-start.3

commit v2 on v1

v2 whole, which is shorter than its diff:
```python
import jax
import jax.numpy as jnp
import numpy as np
from jax import lax
from jax.experimental import pallas as pl
from jax.experimental.pallas import tpu as pltpu
from jax.sharding import Mesh
from jax.sharding import PartitionSpec as P

STEP = 1000


beta_first = 0.9
beta_second = 0.999
adam_epsilon = 1e-08


def moments_step(grad_low, first_moment, second_moment):
    new_first = beta_first * first_moment + (1.0 - beta_first) * grad_low
    new_second = beta_second * second_moment + (1.0 - beta_second) * grad_low * grad_low
    corrected_first = new_first / (1.0 - beta_first**STEP)
    corrected_second = new_second / (1.0 - beta_second**STEP)
    direction = (corrected_first / (jnp.sqrt(corrected_second) + adam_epsilon)).astype(jnp.bfloat16)
    return (new_first, new_second, direction)


CHUNKS = 8


def spread_kernel(terms_ref, spread_ref):
    total = terms_ref[0].astype(jnp.float32)
    for split in range(1, terms_ref.shape[0]):
        total += terms_ref[split].astype(jnp.float32)
    share = total.astype(jnp.bfloat16)

    @pl.loop(0, spread_ref.shape[0])
    def _(chip):
        spread_ref[chip] = share


def sum_and_spread(terms, copies):
    return pl.pallas_call(
        spread_kernel,
        in_specs=[pl.BlockSpec(memory_space=pltpu.VMEM)],
        out_specs=pl.BlockSpec(memory_space=pltpu.VMEM),
        out_shape=jax.ShapeDtypeStruct((copies,) + terms.shape[1:], jnp.bfloat16),
        compiler_params=pltpu.CompilerParams(vmem_limit_bytes=8 * 1024 * 1024),
    )(terms)


def half_dot(side, projected_ref, grad_t_ref, first_chip, chips):
    rows = projected_ref.shape[2]
    at = lambda chip: pl.ds(pl.multiple_of((2 * chip + side) * rows, rows), rows)
    members = range(first_chip, first_chip + chips)
    projected = jnp.concatenate([projected_ref[chip] for chip in members], axis=1)
    grad_t = jnp.concatenate([grad_t_ref[:, at(chip)] for chip in members], axis=1)
    return lax.dot_general(
        grad_t, projected, (((1,), (1,)), ((), ())), preferred_element_type=jnp.float32
    )


def own_kernel(core_ref, own_ref, grad_t_ref, held_ref, partial_ref, sems):
    tokens = grad_t_ref.shape[1] // CHUNKS
    chips = own_ref.shape[0] // CHUNKS
    copies = []
    for chunk in range(CHUNKS):
        part = pl.ds(chunk * tokens, tokens)
        copies.append(
            pltpu.make_async_copy(grad_t_ref.at[:, part], held_ref.at[:, part], sems.at[chunk])
        )
        copies[-1].start()
    total = jnp.zeros(partial_ref.shape, jnp.float32)
    for chunk in range(CHUNKS):
        copies[chunk].wait()
        total += half_dot(core_ref[0], own_ref, held_ref, chunk * chips, chips)
    partial_ref[...] = total


def own_half(core, own, grad_t):
    chips, rank, rows = own.shape
    hidden, tokens = grad_t.shape
    return pl.pallas_call(
        own_kernel,
        in_specs=[
            pl.BlockSpec(memory_space=pltpu.SMEM),
            pl.BlockSpec(memory_space=pltpu.VMEM),
            pl.BlockSpec(memory_space=pltpu.HBM),
        ],
        out_specs=[pl.BlockSpec(memory_space=pltpu.VMEM), pl.BlockSpec(memory_space=pltpu.VMEM)],
        out_shape=[
            jax.ShapeDtypeStruct((hidden, tokens), jnp.bfloat16),
            jax.ShapeDtypeStruct((hidden, rank), jnp.float32),
        ],
        scratch_shapes=[pltpu.SemaphoreType.DMA((CHUNKS,))],
        compiler_params=pltpu.CompilerParams(vmem_limit_bytes=24 * 1024 * 1024),
        cost_estimate=pl.CostEstimate(
            flops=2 * rank * hidden * tokens, bytes_accessed=4 * hidden * tokens, transcendentals=0
        ),
    )(core, own, grad_t)


def moments_kernel(core_ref, other_ref, held_ref, partial_ref, first_ref, second_ref,
                   new_first_ref, new_second_ref, spread_ref, first_in, second_in, sems):
    reads = [
        pltpu.make_async_copy(first_ref, first_in, sems.at[0]),
        pltpu.make_async_copy(second_ref, second_in, sems.at[1]),
    ]
    for read in reads:
        read.start()
    chips = other_ref.shape[0] // CHUNKS
    total = partial_ref[...]
    for chunk in range(CHUNKS):
        total += half_dot(1 - core_ref[0], other_ref, held_ref, chunk * chips, chips)
    for read in reads:
        read.wait()
    new_first, new_second, direction = moments_step(total.T, first_in[...], second_in[...])
    new_first_ref[...] = new_first
    new_second_ref[...] = new_second
    for copy in range(spread_ref.shape[0]):
        spread_ref[copy] = direction


def other_half_and_moments(core, other, held, partial, first_moment, second_moment, copies):
    rank, hidden = first_moment.shape
    vmem = pl.BlockSpec(memory_space=pltpu.VMEM)
    hbm = pl.BlockSpec(memory_space=pltpu.HBM)
    return pl.pallas_call(
        moments_kernel,
        in_specs=[pl.BlockSpec(memory_space=pltpu.SMEM), vmem, vmem, vmem, hbm, hbm],
        out_specs=[vmem, vmem, vmem],
        out_shape=[
            jax.ShapeDtypeStruct((rank, hidden), jnp.float32),
            jax.ShapeDtypeStruct((rank, hidden), jnp.float32),
            jax.ShapeDtypeStruct((copies, rank, hidden), jnp.bfloat16),
        ],
        scratch_shapes=[
            pltpu.VMEM((rank, hidden), jnp.float32),
            pltpu.VMEM((rank, hidden), jnp.float32),
            pltpu.SemaphoreType.DMA((2,)),
        ],
        compiler_params=pltpu.CompilerParams(vmem_limit_bytes=24 * 1024 * 1024),
    )(core, other, held, partial, first_moment, second_moment)


def per_device(acts, out_grad, basis, first_moment, second_moment):
    splits = lax.axis_size("x")
    chips = lax.axis_size("z") * lax.axis_size("y")
    tokens = acts.shape[0]
    rank = basis.shape[1] // splits
    local_terms = lax.dot_general(
        basis, acts, (((0,), (1,)), ((), ())), preferred_element_type=jnp.float32
    ).astype(jnp.bfloat16)
    terms = lax.all_to_all(
        local_terms.reshape(splits, rank, tokens), "x", split_axis=0, concat_axis=0, tiled=True
    )
    spread = sum_and_spread(terms, chips)
    own = lax.all_to_all(spread, ("z", "y"), split_axis=0, concat_axis=0, tiled=True)
    other = lax.ppermute(own, "c", [(0, 1), (1, 0)])
    core = lax.axis_index("c").astype(jnp.int32).reshape(1)
    held, partial = own_half(core, own, pltpu.with_memory_space_constraint(out_grad.T, pltpu.HBM))
    new_first, new_second, direction = other_half_and_moments(
        core, other, held, partial, first_moment, second_moment, splits
    )
    pieces = lax.all_to_all(direction, "x", split_axis=0, concat_axis=0, tiled=True)
    piece = pieces.reshape(splits * rank, pieces.shape[2])
    update = jnp.dot(basis, piece, preferred_element_type=jnp.float32)
    return (update, new_first, new_second)


def solution(mesh):
    chips = Mesh(np.asarray(mesh.devices).reshape(8, 8, 8, 2), ("x", "z", "y", "c"))
    fsdp = ("z", "y", "c")
    return jax.shard_map(
        per_device,
        mesh=chips,
        in_specs=(P(fsdp, "x"), P(None, fsdp), P("x", None), P("x", fsdp), P("x", fsdp)),
        out_specs=(P("x", fsdp), P("x", fsdp), P("x", fsdp)),
        check_vma=False,
    )
```

time: 101 us -> 96.3 us (0.953)
  local copies, waits for them, and re-layouts: 6.23 us -> 1.22 us
  waiting for transfers between devices: 2.26 us -> 0.01 us
  Pallas kernels: 4.58 us -> 6.21 us
    unnamed x8 -> x6, local copies, waits for them, and re-layouts: 5.98 us -> 1.22 us
    ppermute x1, waiting for transfers between devices: 2.26 us -> 0.01 us  [per_device(): other = lax.ppermute(own, 'c', [(0, 1), (1, 0)])]
    pallas_call x1 -> x3, Pallas kernels: 4.58 us -> 6.21 us  [the longest x1 3.77 us: own_half(): pl.pallas_call(own_kernel, in_specs=[pl.BlockSpec(memory_space=pltpu.SMEM...]
  transfers between devices with their start and end apart: 1 -> 1, of which waited for: 1 -> 0; matrix products, arithmetic and copies ran while one was open for 0% -> 0% of each run, Pallas kernels for 0% -> 4%
where the time goes in v2:
time: 96.3 us; the launch traced here: 96 us
  blocking collectives  78.4 us (81%)
  starting transfers between devices  6.6 us (7%)
  Pallas kernels  6.21 us (6%)
  matrix products  2.9 us (3%)
  local copies, waits for them, and re-layouts  1.22 us (1%)
    all_to_all x1, blocking collectives, per_device(): lax.all_to_all(spread, ('z', 'y'), split_axis=0, concat_axis=0, tiled=True)  48.6 us
    all_to_all x1, blocking collectives, per_device(): lax.all_to_all(local_terms.reshape(splits, rank, tokens), 'x', split_axis...  15 us
    all_to_all x1, blocking collectives, per_device(): lax.all_to_all(direction, 'x', split_axis=0, concat_axis=0, tiled=True)  14.8 us
    ppermute x1, starting transfers between devices, per_device(): other = lax.ppermute(own, 'c', [(0, 1), (1, 0)])  6.6 us
    pallas_call x1, Pallas kernels, own_half(): pl.pallas_call(own_kernel, in_specs=[pl.BlockSpec(memory_space=pltpu.SMEM...  3.77 us
    pallas_call x1, Pallas kernels, other_half_and_moments(): pl.pallas_call(moments_kernel, in_specs=[pl.BlockSpec(memory_space=pltpu....  2.09 us
  transfers between devices with their start and end apart: 1, of which 0 were waited for; matrix products, arithmetic and copies ran while one was open for 0% of the time, Pallas kernels for 4%

profile of v2, /device:TPU:1, one launch (start us, length us, event | category | flops | bytes accessed | tf_op | source)
XLA Modules:
  0.0 96.0 jit_solution(14327299808424219148)
XLA Ops:
  0.6 0.0 copy-start
  0.6 0.0 copy-start.2
  0.7 1.2 %copy-done = bf16[1024,512]{1,0:T(8,128)(2,1)S(1)} copy-done((bf16[1024,512]{1,0:T(8,128)(2,1)S(1)}, bf16[1024,512]{1,0:T(8,128)(2,1)}, u32[]{:S(2)}) %copy-start) | copy-done | bytes 1048600
  1.9 0.0 copy-start.1
  1.9 1.5 %convolution_convert_fusion = bf16[512,128]{1,0:T(8,128)(2,1)S(1)} fusion(bf16[1024,512]{1,0:T(8,128)(2,1)S(1)} %copy-done, bf16[128,1024]{1,0:T(8,128)(2,1)} %param.5), kind=kOutput, calls=%fused_computation.1 | convolution fusion | flops 134283264 | bytes 1441792 | tf_op jit(solution)/shard_map/dot_general | solution.py:150
  3.3 15.0 %all_to_all.15.terms_ref = bf16[8,64,128]{2,1,0:T(8,128)(2,1)S(1)} all-to-all(bf16[8,64,128]{2,1,0:T(8,128)(2,1)S(1)} %bitcast.12), channel_id=1, replica_groups=mesh['x'=8,'z'=8,'y'=8,'c'=2] {'x'}, dimensions={0} | all-to-all | bytes 262144 | tf_op jit(solution)/shard_map/all_to_all | solution.py:153
  18.4 0.3 shard_map.76
  18.7 48.6 %all_to_all.16.own_ref = bf16[64,64,128]{2,1,0:T(8,128)(2,1)S(1)} all-to-all(bf16[64,64,128]{2,1,0:T(8,128)(2,1)S(1)} %shard_map.76), channel_id=1, replica_groups=mesh['x'=8,'z'=8,'y'=8,'c'=2] {'z','y'}, dimensions={0} | all-to-all | bytes 2097152 | tf_op jit(solution)/shard_map/all_to_all | solution.py:157
  67.3 6.6 %collective-permute-start = (bf16[64,64,128]{2,1,0:T(8,128)(2,1)S(1)}, bf16[64,64,128]{2,1,0:T(8,128)(2,1)S(1)}, u32[]{:S(2)}, u32[]{:S(2)}) collective-permute-start(bf16[64,64,128]{2,1,0:T(8,128)(2,1)S(1)} %all_to_all.16.own_ref), channel_id=1, source_target_pairs={{0,1},{1,0},{2,3},{3,2},{4,5},{5,4},{6,7},{7,6},{8,9},{9,8},{10,11... | collective-permute-start | bytes 3145736 | tf_op jit(solution)/shard_map/ppermute | solution.py:158
  73.9 3.8 %shard_map.77 = (bf16[224,16384]{1,0:T(8,128)(2,1)S(1)}, f32[224,64]{1,0:T(8,128)S(1)}) custom-call(s32[1]{0:T(128)} %bitcast.core_ref, bf16[64,64,128]{2,1,0:T(8,128)(2,1)S(1)} %all_to_all.16.own_ref, bf16[224,16384]{1,0:T(8,128)(2,1)} %bitcast.10), custom_call_target="tpu_custom_call" | custom-call | flops 469762048 | bytes 14680064 | tf_op jit(solution)/shard_map/pallas_call | solution.py:82
  77.7 0.0 collective-permute-done.other_ref
  77.7 0.0 copy-done.2
  77.7 0.0 copy-done.1
  77.7 2.1 %shard_map.78 = (f32[64,224]{1,0:T(8,128)}, f32[64,224]{1,0:T(8,128)}, bf16[8,64,224]{2,1,0:T(8,128)(2,1)S(1)}) custom-call(s32[1]{0:T(128)} %bitcast.core_ref, bf16[64,64,128]{2,1,0:T(8,128)(2,1)S(1)} %collective-permute-done.other_ref, bf16[224,16384]{1,0:T(8,128)(2,1)S(1)} %get-tuple-element.8.held_ref, f32[224,64]{1,0:T(8,128)S(1)} %get-tuple-element.9.partial_ref, ...), custom_call_target="tpu_custom_call" | custom-call | tf_op jit(solution)/shard_map/pallas_call | solution.py:127
  79.8 14.8 %all_to_all.17 = bf16[8,64,224]{2,1,0:T(8,128)(2,1)S(1)} all-to-all(bf16[8,64,224]{2,1,0:T(8,128)(2,1)S(1)} %get-tuple-element.10), channel_id=1, replica_groups=mesh['x'=8,'z'=8,'y'=8,'c'=2] {'x'}, dimensions={0} | all-to-all | bytes 458752 | tf_op jit(solution)/shard_map/all_to_all | solution.py:164
  94.6 1.4 %convolution_bitcast_fusion = f32[1024,224]{0,1:T(8,128)} fusion(bf16[512,224]{1,0:T(8,128)(2,1)S(1)} %bitcast.11, bf16[1024,512]{1,0:T(8,128)(2,1)S(1)} %copy-done), kind=kOutput, calls=%fused_computation | convolution fusion | flops 234881024 | bytes 2195456 | tf_op jit(solution)/shard_map/dot_general | solution.py:166
Async XLA Ops:
  0.6 1.2 %copy-start = (bf16[1024,512]{1,0:T(8,128)(2,1)S(1)}, bf16[1024,512]{1,0:T(8,128)(2,1)}, u32[]{:S(2)}) copy-start(bf16[1024,512]{1,0:T(8,128)(2,1)} %param.7) | copy-start | bytes 3145732
  0.6 77.0 %copy-start.2 = (f32[64,224]{1,0:T(8,128)S(1)}, f32[64,224]{1,0:T(8,128)}, u32[]{:S(2)}) copy-start(f32[64,224]{1,0:T(8,128)} %second_ref.1) | copy-start | bytes 172036
  1.9 75.8 %copy-start.1 = (f32[64,224]{1,0:T(8,128)S(1)}, f32[64,224]{1,0:T(8,128)}, u32[]{:S(2)}) copy-start(f32[64,224]{1,0:T(8,128)} %first_ref.1) | copy-start | bytes 172036
  67.3 10.4 %collective-permute-start = (bf16[64,64,128]{2,1,0:T(8,128)(2,1)S(1)}, bf16[64,64,128]{2,1,0:T(8,128)(2,1)S(1)}, u32[]{:S(2)}, u32[]{:S(2)}) collective-permute-start(bf16[64,64,128]{2,1,0:T(8,128)(2,1)S(1)} %all_to_all.16.own_ref), channel_id=1, source_target_pairs={{0,1},{1,0},{2,3},{3,2},{4,5},{5,4},{6,7},{7,6},{8,9},{9,8},{10,11... | collective-permute-start | bytes 3145736 | tf_op jit(solution)/shard_map/ppermute | solution.py:158

commit v3 on v2

--- a/solution.py
+++ b/solution.py
@@ -25,6 +25,7 @@
 
 
 CHUNKS = 8
+EARLY = 6
 
 
 def spread_kernel(terms_ref, spread_ref):
@@ -48,9 +49,9 @@
     )(terms)
 
 
-def half_dot(side, projected_ref, grad_t_ref, first_chip, chips):
+def half_dot(side, projected_ref, grad_t_ref, first_chip, chips, skipped=0):
     rows = projected_ref.shape[2]
-    at = lambda chip: pl.ds(pl.multiple_of((2 * chip + side) * rows, rows), rows)
+    at = lambda chip: pl.ds(pl.multiple_of((2 * (chip - skipped) + side) * rows, rows), rows)
     members = range(first_chip, first_chip + chips)
     projected = jnp.concatenate([projected_ref[chip] for chip in members], axis=1)
     grad_t = jnp.concatenate([grad_t_ref[:, at(chip)] for chip in members], axis=1)
@@ -62,16 +63,16 @@
 def own_kernel(core_ref, own_ref, grad_t_ref, held_ref, partial_ref, sems):
     tokens = grad_t_ref.shape[1] // CHUNKS
     chips = own_ref.shape[0] // CHUNKS
-    copies = []
-    for chunk in range(CHUNKS):
+    reads = []
+    for chunk in range(EARLY):
         part = pl.ds(chunk * tokens, tokens)
-        copies.append(
+        reads.append(
             pltpu.make_async_copy(grad_t_ref.at[:, part], held_ref.at[:, part], sems.at[chunk])
         )
-        copies[-1].start()
+        reads[-1].start()
     total = jnp.zeros(partial_ref.shape, jnp.float32)
-    for chunk in range(CHUNKS):
-        copies[chunk].wait()
+    for chunk in range(EARLY):
+        reads[chunk].wait()
         total += half_dot(core_ref[0], own_ref, held_ref, chunk * chips, chips)
     partial_ref[...] = total
 
@@ -88,30 +89,42 @@
         ],
         out_specs=[pl.BlockSpec(memory_space=pltpu.VMEM), pl.BlockSpec(memory_space=pltpu.VMEM)],
         out_shape=[
-            jax.ShapeDtypeStruct((hidden, tokens), jnp.bfloat16),
+            jax.ShapeDtypeStruct((hidden, tokens * EARLY // CHUNKS), jnp.bfloat16),
             jax.ShapeDtypeStruct((hidden, rank), jnp.float32),
         ],
-        scratch_shapes=[pltpu.SemaphoreType.DMA((CHUNKS,))],
+        scratch_shapes=[pltpu.SemaphoreType.DMA((EARLY,))],
         compiler_params=pltpu.CompilerParams(vmem_limit_bytes=24 * 1024 * 1024),
         cost_estimate=pl.CostEstimate(
-            flops=2 * rank * hidden * tokens, bytes_accessed=4 * hidden * tokens, transcendentals=0
+            flops=rank * hidden * tokens, bytes_accessed=2 * hidden * tokens, transcendentals=0
         ),
     )(core, own, grad_t)
 
 
-def moments_kernel(core_ref, other_ref, held_ref, partial_ref, first_ref, second_ref,
-                   new_first_ref, new_second_ref, spread_ref, first_in, second_in, sems):
-    reads = [
-        pltpu.make_async_copy(first_ref, first_in, sems.at[0]),
-        pltpu.make_async_copy(second_ref, second_in, sems.at[1]),
-    ]
+def moments_kernel(core_ref, own_ref, other_ref, held_ref, grad_t_ref, partial_ref, first_ref, second_ref,
+                   new_first_ref, new_second_ref, spread_ref, late_ref, first_in, second_in, sems):
+    chips = other_ref.shape[0] // CHUNKS
+    tokens = grad_t_ref.shape[1] // CHUNKS
+    reads = []
+    for chunk in range(EARLY, CHUNKS):
+        part = pl.ds((chunk - EARLY) * tokens, tokens)
+        reads.append(
+            pltpu.make_async_copy(
+                grad_t_ref.at[:, pl.ds(chunk * tokens, tokens)], late_ref.at[:, part], sems.at[chunk - EARLY]
+            )
+        )
+    reads.append(pltpu.make_async_copy(first_ref, first_in, sems.at[CHUNKS - EARLY]))
+    reads.append(pltpu.make_async_copy(second_ref, second_in, sems.at[CHUNKS - EARLY + 1]))
     for read in reads:
         read.start()
-    chips = other_ref.shape[0] // CHUNKS
+    side = core_ref[0]
     total = partial_ref[...]
-    for chunk in range(CHUNKS):
-        total += half_dot(1 - core_ref[0], other_ref, held_ref, chunk * chips, chips)
-    for read in reads:
+    for chunk in range(EARLY):
+        total += half_dot(1 - side, other_ref, held_ref, chunk * chips, chips)
+    for chunk in range(EARLY, CHUNKS):
+        reads[chunk - EARLY].wait()
+        total += half_dot(side, own_ref, late_ref, chunk * chips, chips, EARLY * chips)
+        total += half_dot(1 - side, other_ref, late_ref, chunk * chips, chips, EARLY * chips)
+    for read in reads[CHUNKS - EARLY :]:
         read.wait()
     new_first, new_second, direction = moments_step(total.T, first_in[...], second_in[...])
     new_first_ref[...] = new_first
@@ -120,13 +133,13 @@
         spread_ref[copy] = direction
 
 
-def other_half_and_moments(core, other, held, partial, first_moment, second_moment, copies):
+def rest_and_moments(core, own, other, held, grad_t, partial, first_moment, second_moment, copies):
     rank, hidden = first_moment.shape
     vmem = pl.BlockSpec(memory_space=pltpu.VMEM)
     hbm = pl.BlockSpec(memory_space=pltpu.HBM)
     return pl.pallas_call(
         moments_kernel,
-        in_specs=[pl.BlockSpec(memory_space=pltpu.SMEM), vmem, vmem, vmem, hbm, hbm],
+        in_specs=[pl.BlockSpec(memory_space=pltpu.SMEM), vmem, vmem, vmem, hbm, vmem, hbm, hbm],
         out_specs=[vmem, vmem, vmem],
         out_shape=[
             jax.ShapeDtypeStruct((rank, hidden), jnp.float32),
@@ -134,12 +147,55 @@
             jax.ShapeDtypeStruct((copies, rank, hidden), jnp.bfloat16),
         ],
         scratch_shapes=[
+            pltpu.VMEM((hidden, grad_t.shape[1] * (CHUNKS - EARLY) // CHUNKS), jnp.bfloat16),
             pltpu.VMEM((rank, hidden), jnp.float32),
             pltpu.VMEM((rank, hidden), jnp.float32),
-            pltpu.SemaphoreType.DMA((2,)),
+            pltpu.SemaphoreType.DMA((CHUNKS - EARLY + 2,)),
         ],
         compiler_params=pltpu.CompilerParams(vmem_limit_bytes=24 * 1024 * 1024),
-    )(core, other, held, partial, first_moment, second_moment)
+    )(core, own, other, held, grad_t, partial, first_moment, second_moment)
+
+
+PARTS = 4
+
+
+def project_kernel(acts_ref, basis_ref, terms_ref, acts_in, basis_in, sems):
+    depth = acts_ref.shape[1] // PARTS
+    reads = []
+    for part in range(PARTS):
+        at = pl.ds(part * depth, depth)
+        reads.append(
+            (
+                pltpu.make_async_copy(acts_ref.at[:, at], acts_in.at[:, at], sems.at[0, part]),
+                pltpu.make_async_copy(basis_ref.at[at, :], basis_in.at[at, :], sems.at[1, part]),
+            )
+        )
+        for read in reads[-1]:
+            read.start()
+    total = jnp.zeros((acts_ref.shape[0], basis_ref.shape[1]), jnp.float32)
+    for part in range(PARTS):
+        for read in reads[part]:
+            read.wait()
+        at = pl.ds(part * depth, depth)
+        total += jnp.dot(acts_in[:, at], basis_in[at, :], preferred_element_type=jnp.float32)
+    terms_ref[...] = total.T.astype(jnp.bfloat16)
+
+
+def project(acts, basis):
+    tokens, ranks = acts.shape[0], basis.shape[1]
+    hbm = pl.BlockSpec(memory_space=pltpu.HBM)
+    return pl.pallas_call(
+        project_kernel,
+        in_specs=[hbm, hbm],
+        out_specs=pl.BlockSpec(memory_space=pltpu.VMEM),
+        out_shape=jax.ShapeDtypeStruct((ranks, tokens), jnp.bfloat16),
+        scratch_shapes=[
+            pltpu.VMEM(acts.shape, jnp.bfloat16),
+            pltpu.VMEM(basis.shape, jnp.bfloat16),
+            pltpu.SemaphoreType.DMA((2, PARTS)),
+        ],
+        compiler_params=pltpu.CompilerParams(vmem_limit_bytes=16 * 1024 * 1024),
+    )(acts, basis)
 
 
 def per_device(acts, out_grad, basis, first_moment, second_moment):
@@ -147,9 +203,9 @@
     chips = lax.axis_size("z") * lax.axis_size("y")
     tokens = acts.shape[0]
     rank = basis.shape[1] // splits
-    local_terms = lax.dot_general(
-        basis, acts, (((0,), (1,)), ((), ())), preferred_element_type=jnp.float32
-    ).astype(jnp.bfloat16)
+    in_hbm = lambda array: pltpu.with_memory_space_constraint(array, pltpu.HBM)
+    grad_t = in_hbm(out_grad.T)
+    local_terms = project(in_hbm(acts), in_hbm(basis))
     terms = lax.all_to_all(
         local_terms.reshape(splits, rank, tokens), "x", split_axis=0, concat_axis=0, tiled=True
     )
@@ -157,9 +213,9 @@
     own = lax.all_to_all(spread, ("z", "y"), split_axis=0, concat_axis=0, tiled=True)
     other = lax.ppermute(own, "c", [(0, 1), (1, 0)])
     core = lax.axis_index("c").astype(jnp.int32).reshape(1)
-    held, partial = own_half(core, own, pltpu.with_memory_space_constraint(out_grad.T, pltpu.HBM))
-    new_first, new_second, direction = other_half_and_moments(
-        core, other, held, partial, first_moment, second_moment, splits
+    held, partial = own_half(core, own, grad_t)
+    new_first, new_second, direction = rest_and_moments(
+        core, own, other, held, grad_t, partial, first_moment, second_moment, splits
     )
     pieces = lax.all_to_all(direction, "x", split_axis=0, concat_axis=0, tiled=True)
     piece = pieces.reshape(splits * rank, pieces.shape[2])

time: 96.3 us -> 96.2 us (level)
  Pallas kernels: 6.21 us -> 8.64 us
  matrix products: 2.9 us -> 1.44 us
  local copies, waits for them, and re-layouts: 1.22 us -> 0.01 us
    pallas_call x1 -> x2, Pallas kernels: 2.09 us -> 5.05 us  [the longest x1 3.37 us: rest_and_moments(): pl.pallas_call(moments_kernel, in_specs=[pl.BlockSpec(memory_space=pltpu....]
    dot_general x1 -> x0, matrix products: 1.46 us -> none  [per_device(): lax.dot_general(basis, acts, (((0,), (1,)), ((), ())), preferred_element_...]
    unnamed x6, local copies, waits for them, and re-layouts: 1.22 us -> 0.01 us
  transfers between devices with their start and end apart: 1 -> 1, of which waited for: 0 -> 0; matrix products, arithmetic and copies ran while one was open for 0% -> 0% of each run, Pallas kernels for 4% -> 3%
where the time goes in v3:
time: 96.2 us; the launch traced here: 96 us
  blocking collectives  78.5 us (82%)
  Pallas kernels  8.64 us (9%)
  starting transfers between devices  6.62 us (7%)
  matrix products  1.44 us (1%)
    all_to_all x1, blocking collectives, per_device(): lax.all_to_all(spread, ('z', 'y'), split_axis=0, concat_axis=0, tiled=True)  48.7 us
    all_to_all x1, blocking collectives, per_device(): lax.all_to_all(local_terms.reshape(splits, rank, tokens), 'x', split_axis...  15 us
    all_to_all x1, blocking collectives, per_device(): lax.all_to_all(direction, 'x', split_axis=0, concat_axis=0, tiled=True)  14.8 us
    ppermute x1, starting transfers between devices, per_device(): other = lax.ppermute(own, 'c', [(0, 1), (1, 0)])  6.62 us
    pallas_call x1, Pallas kernels, rest_and_moments(): pl.pallas_call(moments_kernel, in_specs=[pl.BlockSpec(memory_space=pltpu....  3.37 us
    pallas_call x1, Pallas kernels, own_half(): pl.pallas_call(own_kernel, in_specs=[pl.BlockSpec(memory_space=pltpu.SMEM...  3.25 us
  transfers between devices with their start and end apart: 1, of which 0 were waited for; matrix products, arithmetic and copies ran while one was open for 0% of the time, Pallas kernels for 3%

profile of v3, /device:TPU:1, one launch (start us, length us, event | category | flops | bytes accessed | tf_op | source)
XLA Modules:
  0.0 96.0 jit_solution(8453359106352794823)
XLA Ops:
  0.6 0.0 copy-start.1
  0.6 0.0 copy-start
  0.7 1.7 %shard_map.76 = bf16[512,128]{1,0:T(8,128)(2,1)S(1)} custom-call(bf16[128,1024]{1,0:T(8,128)(2,1)} %acts_ref.1, bf16[1024,512]{1,0:T(8,128)(2,1)} %basis_ref.1), custom_call_target="tpu_custom_call" | custom-call | tf_op jit(solution)/shard_map/pallas_call | solution.py:187
  2.3 15.0 %all_to_all.15.terms_ref = bf16[8,64,128]{2,1,0:T(8,128)(2,1)S(1)} all-to-all(bf16[8,64,128]{2,1,0:T(8,128)(2,1)S(1)} %bitcast.8), channel_id=1, replica_groups=mesh['x'=8,'z'=8,'y'=8,'c'=2] {'x'}, dimensions={0} | all-to-all | bytes 262144 | tf_op jit(solution)/shard_map/all_to_all | solution.py:209
  17.4 0.3 shard_map.77
  17.7 48.7 %all_to_all.16.own_ref = bf16[64,64,128]{2,1,0:T(8,128)(2,1)S(1)} all-to-all(bf16[64,64,128]{2,1,0:T(8,128)(2,1)S(1)} %shard_map.77), channel_id=1, replica_groups=mesh['x'=8,'z'=8,'y'=8,'c'=2] {'z','y'}, dimensions={0} | all-to-all | bytes 2097152 | tf_op jit(solution)/shard_map/all_to_all | solution.py:213
  66.4 6.6 %collective-permute-start = (bf16[64,64,128]{2,1,0:T(8,128)(2,1)S(1)}, bf16[64,64,128]{2,1,0:T(8,128)(2,1)S(1)}, u32[]{:S(2)}, u32[]{:S(2)}) collective-permute-start(bf16[64,64,128]{2,1,0:T(8,128)(2,1)S(1)} %all_to_all.16.own_ref), channel_id=1, source_target_pairs={{0,1},{1,0},{2,3},{3,2},{4,5},{5,4},{6,7},{7,6},{8,9},{9,8},{10,11... | collective-permute-start | bytes 3145736 | tf_op jit(solution)/shard_map/ppermute | solution.py:214
  73.1 3.2 %shard_map.78 = (bf16[224,12288]{1,0:T(8,128)(2,1)S(1)}, f32[224,64]{1,0:T(8,128)S(1)}) custom-call(s32[1]{0:T(128)} %bitcast.core_ref, bf16[64,64,128]{2,1,0:T(8,128)(2,1)S(1)} %all_to_all.16.own_ref, bf16[224,16384]{1,0:T(8,128)(2,1)} %bitcast.9), custom_call_target="tpu_custom_call" | custom-call | flops 234881024 | bytes 7340032 | tf_op jit(solution)/shard_map/pallas_call | solution.py:83
  76.3 0.0 collective-permute-done.other_ref
  76.3 0.0 copy-done.1
  76.3 0.0 copy-done
  76.4 0.0 copy-start.2
  76.4 3.4 %shard_map.79 = (f32[64,224]{1,0:T(8,128)}, f32[64,224]{1,0:T(8,128)}, bf16[8,64,224]{2,1,0:T(8,128)(2,1)S(1)}) custom-call(s32[1]{0:T(128)} %bitcast.core_ref, bf16[64,64,128]{2,1,0:T(8,128)(2,1)S(1)} %all_to_all.16.own_ref, bf16[64,64,128]{2,1,0:T(8,128)(2,1)S(1)} %collective-permute-done.other_ref, bf16[224,12288]{1,0:T(8,128)(2,1)S(1)} %get-tuple-element.8.held_ref, ...), custom_call_target="tpu_custom_call" | custom-call | tf_op jit(solution)/shard_map/pallas_call | solution.py:140
  79.8 14.8 %all_to_all.17 = bf16[8,64,224]{2,1,0:T(8,128)(2,1)S(1)} all-to-all(bf16[8,64,224]{2,1,0:T(8,128)(2,1)S(1)} %get-tuple-element.10), channel_id=1, replica_groups=mesh['x'=8,'z'=8,'y'=8,'c'=2] {'x'}, dimensions={0} | all-to-all | bytes 458752 | tf_op jit(solution)/shard_map/all_to_all | solution.py:220
  94.5 0.0 copy-done.2
  94.5 1.4 %convolution_bitcast_fusion = f32[1024,224]{0,1:T(8,128)} fusion(bf16[512,224]{1,0:T(8,128)(2,1)S(1)} %bitcast.11, bf16[1024,512]{1,0:T(8,128)(2,1)S(1)} %copy-done.2), kind=kOutput, calls=%fused_computation | convolution fusion | flops 234881024 | bytes 2195456 | tf_op jit(solution)/shard_map/dot_general | solution.py:222
Async XLA Ops:
  0.6 75.7 %copy-start.1 = (f32[64,224]{1,0:T(8,128)S(1)}, f32[64,224]{1,0:T(8,128)}, u32[]{:S(2)}) copy-start(f32[64,224]{1,0:T(8,128)} %second_ref.1) | copy-start | bytes 172036
  0.6 75.7 %copy-start = (f32[64,224]{1,0:T(8,128)S(1)}, f32[64,224]{1,0:T(8,128)}, u32[]{:S(2)}) copy-start(f32[64,224]{1,0:T(8,128)} %first_ref.1) | copy-start | bytes 172036
  66.4 9.9 %collective-permute-start = (bf16[64,64,128]{2,1,0:T(8,128)(2,1)S(1)}, bf16[64,64,128]{2,1,0:T(8,128)(2,1)S(1)}, u32[]{:S(2)}, u32[]{:S(2)}) collective-permute-start(bf16[64,64,128]{2,1,0:T(8,128)(2,1)S(1)} %all_to_all.16.own_ref), channel_id=1, source_target_pairs={{0,1},{1,0},{2,3},{3,2},{4,5},{5,4},{6,7},{7,6},{8,9},{9,8},{10,11... | collective-permute-start | bytes 3145736 | tf_op jit(solution)/shard_map/ppermute | solution.py:214
  76.4 18.2 %copy-start.2 = (bf16[1024,512]{1,0:T(8,128)(2,1)S(1)}, bf16[1024,512]{1,0:T(8,128)(2,1)}, u32[]{:S(2)}) copy-start(bf16[1024,512]{1,0:T(8,128)(2,1)} %basis_ref.1) | copy-start | bytes 3145732

commit v4 on v2

--- a/solution.py
+++ b/solution.py
@@ -1,10 +1,8 @@
 import jax
 import jax.numpy as jnp
-import numpy as np
 from jax import lax
 from jax.experimental import pallas as pl
 from jax.experimental.pallas import tpu as pltpu
-from jax.sharding import Mesh
 from jax.sharding import PartitionSpec as P
 
 STEP = 1000
@@ -25,6 +23,8 @@
 
 
 CHUNKS = 8
+SIDE = 8
+CORES = 2
 
 
 def spread_kernel(terms_ref, spread_ref):
@@ -52,7 +52,8 @@
     rows = projected_ref.shape[2]
     at = lambda chip: pl.ds(pl.multiple_of((2 * chip + side) * rows, rows), rows)
     members = range(first_chip, first_chip + chips)
-    projected = jnp.concatenate([projected_ref[chip] for chip in members], axis=1)
+    place = lambda chip: jnp.where(side == 0, chip, chip % SIDE * SIDE + chip // SIDE)
+    projected = jnp.concatenate([projected_ref[place(chip)] for chip in members], axis=1)
     grad_t = jnp.concatenate([grad_t_ref[:, at(chip)] for chip in members], axis=1)
     return lax.dot_general(
         grad_t, projected, (((1,), (1,)), ((), ())), preferred_element_type=jnp.float32
@@ -142,38 +143,101 @@
     )(core, other, held, partial, first_moment, second_moment)
 
 
+PARTS = 4
+
+
+def project_kernel(acts_ref, basis_ref, terms_ref, acts_in, basis_in, sems):
+    depth = acts_ref.shape[1] // PARTS
+    reads = []
+    for part in range(PARTS):
+        at = pl.ds(part * depth, depth)
+        reads.append(
+            (
+                pltpu.make_async_copy(acts_ref.at[:, at], acts_in.at[:, at], sems.at[0, part]),
+                pltpu.make_async_copy(basis_ref.at[at, :], basis_in.at[at, :], sems.at[1, part]),
+            )
+        )
+        for read in reads[-1]:
+            read.start()
+    total = jnp.zeros((acts_ref.shape[0], basis_ref.shape[1]), jnp.float32)
+    for part in range(PARTS):
+        for read in reads[part]:
+            read.wait()
+        at = pl.ds(part * depth, depth)
+        total += jnp.dot(acts_in[:, at], basis_in[at, :], preferred_element_type=jnp.float32)
+    terms_ref[...] = total.T.astype(jnp.bfloat16)
+
+
+def project(acts, basis):
+    tokens, ranks = acts.shape[0], basis.shape[1]
+    hbm = pl.BlockSpec(memory_space=pltpu.HBM)
+    return pl.pallas_call(
+        project_kernel,
+        in_specs=[hbm, hbm],
+        out_specs=pl.BlockSpec(memory_space=pltpu.VMEM),
+        out_shape=jax.ShapeDtypeStruct((ranks, tokens), jnp.bfloat16),
+        scratch_shapes=[
+            pltpu.VMEM(acts.shape, jnp.bfloat16),
+            pltpu.VMEM(basis.shape, jnp.bfloat16),
+            pltpu.SemaphoreType.DMA((2, PARTS)),
+        ],
+        compiler_params=pltpu.CompilerParams(vmem_limit_bytes=16 * 1024 * 1024),
+    )(acts, basis)
+
+
+def crossing(first):
+    groups = []
+    for at in range(SIDE):
+        groups.append([(z * SIDE + at) * CORES + first for z in range(SIDE)])
+        groups.append([(at * SIDE + y) * CORES + 1 - first for y in range(SIDE)])
+    return groups
+
+
+def exchange(block, first):
+    copies = jnp.broadcast_to(block[None], (SIDE,) + block.shape)
+    return lax.all_to_all(
+        copies, "fsdp", split_axis=0, concat_axis=0, tiled=True, axis_index_groups=crossing(first)
+    )
+
+
 def per_device(acts, out_grad, basis, first_moment, second_moment):
-    splits = lax.axis_size("x")
-    chips = lax.axis_size("z") * lax.axis_size("y")
+    splits = lax.axis_size("dp")
     tokens = acts.shape[0]
     rank = basis.shape[1] // splits
-    local_terms = lax.dot_general(
-        basis, acts, (((0,), (1,)), ((), ())), preferred_element_type=jnp.float32
-    ).astype(jnp.bfloat16)
+    in_hbm = lambda array: pltpu.with_memory_space_constraint(array, pltpu.HBM)
+    grad_t = in_hbm(out_grad.T)
+    local_terms = project(in_hbm(acts), in_hbm(basis))
     terms = lax.all_to_all(
-        local_terms.reshape(splits, rank, tokens), "x", split_axis=0, concat_axis=0, tiled=True
-    )
-    spread = sum_and_spread(terms, chips)
-    own = lax.all_to_all(spread, ("z", "y"), split_axis=0, concat_axis=0, tiled=True)
-    other = lax.ppermute(own, "c", [(0, 1), (1, 0)])
-    core = lax.axis_index("c").astype(jnp.int32).reshape(1)
-    held, partial = own_half(core, own, pltpu.with_memory_space_constraint(out_grad.T, pltpu.HBM))
+        local_terms.reshape(splits, rank, tokens), "dp", split_axis=0, concat_axis=0, tiled=True
+    )
+    line = lax.all_to_all(
+        sum_and_spread(terms, SIDE), "fsdp", split_axis=0, concat_axis=0, tiled=True,
+        axis_index_groups=crossing(1),
+    )
+    own = exchange(line, 0).reshape(SIDE * SIDE, rank, tokens)
+    other = lax.ppermute(own, "fsdp", [(at, at ^ 1) for at in range(SIDE * SIDE * CORES)])
+    core = (lax.axis_index("fsdp") & (CORES - 1)).astype(jnp.int32).reshape(1)
+    held, partial = own_half(core, own, grad_t)
     new_first, new_second, direction = other_half_and_moments(
         core, other, held, partial, first_moment, second_moment, splits
     )
-    pieces = lax.all_to_all(direction, "x", split_axis=0, concat_axis=0, tiled=True)
+    pieces = lax.all_to_all(direction, "dp", split_axis=0, concat_axis=0, tiled=True)
     piece = pieces.reshape(splits * rank, pieces.shape[2])
     update = jnp.dot(basis, piece, preferred_element_type=jnp.float32)
     return (update, new_first, new_second)
 
 
 def solution(mesh):
-    chips = Mesh(np.asarray(mesh.devices).reshape(8, 8, 8, 2), ("x", "z", "y", "c"))
-    fsdp = ("z", "y", "c")
     return jax.shard_map(
         per_device,
-        mesh=chips,
-        in_specs=(P(fsdp, "x"), P(None, fsdp), P("x", None), P("x", fsdp), P("x", fsdp)),
-        out_specs=(P("x", fsdp), P("x", fsdp), P("x", fsdp)),
+        mesh=mesh,
+        in_specs=(
+            P("fsdp", "dp"),
+            P(None, "fsdp"),
+            P("dp", None),
+            P("dp", "fsdp"),
+            P("dp", "fsdp"),
+        ),
+        out_specs=(P("dp", "fsdp"), P("dp", "fsdp"), P("dp", "fsdp")),
         check_vma=False,
     )

time: 96.3 us -> 96.3 us (level)
  Pallas kernels: 6.21 us -> 7.71 us
  matrix products: 2.9 us -> 1.44 us
    pallas_call x0 -> x1, Pallas kernels: none -> 1.67 us  [project(): pl.pallas_call(project_kernel, in_specs=[hbm, hbm], out_specs=pl.BlockSpe...]
    dot_general x1 -> x0, matrix products: 1.46 us -> none  [per_device(): lax.dot_general(basis, acts, (((0,), (1,)), ((), ())), preferred_element_...]
    unnamed x6, local copies, waits for them, and re-layouts: 1.22 us -> 0.01 us
    all_to_all x3 -> x4, blocking collectives: 78.4 us -> 78.8 us  [the longest x1 25 us: exchange(): lax.all_to_all(copies, 'fsdp', split_axis=0, concat_axis=0, tiled=True, a...]
where the time goes in v4:
time: 96.3 us; the launch traced here: 96 us
  blocking collectives  78.8 us (82%)
  Pallas kernels  7.71 us (8%)
  starting transfers between devices  7.04 us (7%)
  matrix products  1.44 us (1%)
    all_to_all x1, blocking collectives, exchange(): lax.all_to_all(copies, 'fsdp', split_axis=0, concat_axis=0, tiled=True, a...  25 us
    all_to_all x1, blocking collectives, per_device(): lax.all_to_all(sum_and_spread(terms, SIDE), 'fsdp', split_axis=0, concat_...  24 us
    all_to_all x1, blocking collectives, per_device(): lax.all_to_all(local_terms.reshape(splits, rank, tokens), 'dp', split_axi...  15 us
    all_to_all x1, blocking collectives, per_device(): lax.all_to_all(direction, 'dp', split_axis=0, concat_axis=0, tiled=True)  14.8 us
    ppermute x1, starting transfers between devices, per_device(): lax.ppermute(own, 'fsdp', [(at, at ^ 1) for at in range(SIDE * SIDE * COR...  7.04 us
    pallas_call x1, Pallas kernels, own_half(): pl.pallas_call(own_kernel, in_specs=[pl.BlockSpec(memory_space=pltpu.SMEM...  3.86 us
    pallas_call x1, Pallas kernels, other_half_and_moments(): pl.pallas_call(moments_kernel, in_specs=[pl.BlockSpec(memory_space=pltpu....  2.12 us
  transfers between devices with their start and end apart: 1, of which 0 were waited for; matrix products, arithmetic and copies ran while one was open for 0% of the time, Pallas kernels for 4%

profile of v4, /device:TPU:1, one launch (start us, length us, event | category | flops | bytes accessed | tf_op | source)
XLA Modules:
  0.0 96.0 jit_solution(15728505533774296702)
XLA Ops:
  0.6 0.0 copy-start.1
  0.6 0.0 copy-start
  0.7 1.7 %shard_map.76 = bf16[512,128]{1,0:T(8,128)(2,1)S(1)} custom-call(bf16[128,1024]{1,0:T(8,128)(2,1)} %acts_ref.1, bf16[1024,512]{1,0:T(8,128)(2,1)} %basis_ref.1), custom_call_target="tpu_custom_call" | custom-call | tf_op jit(solution)/shard_map/pallas_call | solution.py:174
  2.3 15.0 %all_to_all.20.terms_ref = bf16[8,64,128]{2,1,0:T(8,128)(2,1)S(1)} all-to-all(bf16[8,64,128]{2,1,0:T(8,128)(2,1)S(1)} %bitcast.11), channel_id=1, replica_groups=mesh['dp'=8,'fsdp'=128] {'dp'}, dimensions={0} | all-to-all | bytes 262144 | tf_op jit(solution)/shard_map/all_to_all | solution.py:210
  17.4 0.1 shard_map.77
  17.4 24.0 %all_to_all.21 = bf16[8,64,128]{2,1,0:T(8,128)(2,1)S(1)} all-to-all(bf16[8,64,128]{2,1,0:T(8,128)(2,1)S(1)} %shard_map.77), channel_id=1, replica_groups={{1,17,33,49,65,81,97,113},{0,2,4,6,8,10,12,14},{3,19,35,51,67,83,99,115..., dimensions={0} | all-to-all | bytes 262144 | tf_op jit(solution)/shard_map/all_to_all | solution.py:213
  41.4 0.2 broadcast_in_dim.2
  41.7 25.0 %all_to_all.22 = bf16[8,8,64,128]{3,2,1,0:T(8,128)(2,1)S(1)} all-to-all(bf16[8,8,64,128]{3,2,1,0:T(8,128)(2,1)S(1)} %broadcast_in_dim.2), channel_id=1, replica_groups={{0,16,32,48,64,80,96,112},{1,3,5,7,9,11,13,15},{2,18,34,50,66,82,98,114..., dimensions={0} | all-to-all | bytes 2097152 | tf_op jit(solution)/shard_map/all_to_all | solution.py:198
  66.7 7.0 %collective-permute-start = (bf16[64,64,128]{2,1,0:T(8,128)(2,1)S(1)}, bf16[64,64,128]{2,1,0:T(8,128)(2,1)S(1)}, u32[]{:S(2)}, u32[]{:S(2)}) collective-permute-start(bf16[64,64,128]{2,1,0:T(8,128)(2,1)S(1)} %bitcast.9), channel_id=1, source_target_pairs={{0,1},{1,0},{2,3},{3,2},{4,5},{5,4},{6,7},{7,6},{8,9},{9,8},{10,11... | collective-permute-start | bytes 3145736 | tf_op jit(solution)/shard_map/ppermute | solution.py:218
  73.7 0.0 copy-start.2
  73.7 3.9 %shard_map.78 = (bf16[224,16384]{1,0:T(8,128)(2,1)S(1)}, f32[224,64]{1,0:T(8,128)S(1)}) custom-call(s32[1]{0:T(128)} %bitcast.core_ref, bf16[64,64,128]{2,1,0:T(8,128)(2,1)S(1)} %bitcast.10, bf16[224,16384]{1,0:T(8,128)(2,1)} %bitcast.12), custom_call_target="tpu_custom_call" | custom-call | flops 469762048 | bytes 14680064 | tf_op jit(solution)/shard_map/pallas_call | solution.py:83
  77.6 0.0 collective-permute-done.other_ref
  77.6 0.0 copy-done.1
  77.6 0.0 copy-done
  77.6 2.1 %shard_map.79 = (f32[64,224]{1,0:T(8,128)}, f32[64,224]{1,0:T(8,128)}, bf16[8,64,224]{2,1,0:T(8,128)(2,1)S(1)}) custom-call(s32[1]{0:T(128)} %bitcast.core_ref, bf16[64,64,128]{2,1,0:T(8,128)(2,1)S(1)} %collective-permute-done.other_ref, bf16[224,16384]{1,0:T(8,128)(2,1)S(1)} %get-tuple-element.8.held_ref, f32[224,64]{1,0:T(8,128)S(1)} %get-tuple-element.9.partial_ref, ...), custom_call_target="tpu_custom_call" | custom-call | tf_op jit(solution)/shard_map/pallas_call | solution.py:128
  79.8 14.8 %all_to_all.23 = bf16[8,64,224]{2,1,0:T(8,128)(2,1)S(1)} all-to-all(bf16[8,64,224]{2,1,0:T(8,128)(2,1)S(1)} %get-tuple-element.10), channel_id=1, replica_groups=mesh['dp'=8,'fsdp'=128] {'dp'}, dimensions={0} | all-to-all | bytes 458752 | tf_op jit(solution)/shard_map/all_to_all | solution.py:224
  94.6 0.0 copy-done.2
  94.6 1.4 %convolution_bitcast_fusion = f32[1024,224]{0,1:T(8,128)} fusion(bf16[512,224]{1,0:T(8,128)(2,1)S(1)} %bitcast.13, bf16[1024,512]{1,0:T(8,128)(2,1)S(1)} %copy-done.2), kind=kOutput, calls=%fused_computation | convolution fusion | flops 234881024 | bytes 2195456 | tf_op jit(solution)/shard_map/dot_general | solution.py:226
Async XLA Ops:
  0.6 77.0 %copy-start.1 = (f32[64,224]{1,0:T(8,128)S(1)}, f32[64,224]{1,0:T(8,128)}, u32[]{:S(2)}) copy-start(f32[64,224]{1,0:T(8,128)} %second_ref.1) | copy-start | bytes 172036
  0.6 77.0 %copy-start = (f32[64,224]{1,0:T(8,128)S(1)}, f32[64,224]{1,0:T(8,128)}, u32[]{:S(2)}) copy-start(f32[64,224]{1,0:T(8,128)} %first_ref.1) | copy-start | bytes 172036
  66.7 10.9 %collective-permute-start = (bf16[64,64,128]{2,1,0:T(8,128)(2,1)S(1)}, bf16[64,64,128]{2,1,0:T(8,128)(2,1)S(1)}, u32[]{:S(2)}, u32[]{:S(2)}) collective-permute-start(bf16[64,64,128]{2,1,0:T(8,128)(2,1)S(1)} %bitcast.9), channel_id=1, source_target_pairs={{0,1},{1,0},{2,3},{3,2},{4,5},{5,4},{6,7},{7,6},{8,9},{9,8},{10,11... | collective-permute-start | bytes 3145736 | tf_op jit(solution)/shard_map/ppermute | solution.py:218
  73.7 20.8 %copy-start.2 = (bf16[1024,512]{1,0:T(8,128)(2,1)S(1)}, bf16[1024,512]{1,0:T(8,128)(2,1)}, u32[]{:S(2)}) copy-start(bf16[1024,512]{1,0:T(8,128)(2,1)} %basis_ref.1) | copy-start | bytes 3145732

commit v5 on v2

--- a/solution.py
+++ b/solution.py
@@ -142,14 +142,56 @@
     )(core, other, held, partial, first_moment, second_moment)
 
 
+PARTS = 4
+
+
+def project_kernel(acts_ref, basis_ref, terms_ref, acts_in, basis_in, sems):
+    depth = acts_ref.shape[1] // PARTS
+    reads = []
+    for part in range(PARTS):
+        at = pl.ds(part * depth, depth)
+        reads.append(
+            (
+                pltpu.make_async_copy(acts_ref.at[:, at], acts_in.at[:, at], sems.at[0, part]),
+                pltpu.make_async_copy(basis_ref.at[at, :], basis_in.at[at, :], sems.at[1, part]),
+            )
+        )
+        for read in reads[-1]:
+            read.start()
+    total = jnp.zeros((acts_ref.shape[0], basis_ref.shape[1]), jnp.float32)
+    for part in range(PARTS):
+        for read in reads[part]:
+            read.wait()
+        at = pl.ds(part * depth, depth)
+        total += jnp.dot(acts_in[:, at], basis_in[at, :], preferred_element_type=jnp.float32)
+    terms_ref[...] = total.T.astype(jnp.bfloat16)
+
+
+def project(acts, basis):
+    tokens, ranks = acts.shape[0], basis.shape[1]
+    hbm = pl.BlockSpec(memory_space=pltpu.HBM)
+    return pl.pallas_call(
+        project_kernel,
+        in_specs=[hbm, hbm],
+        out_specs=pl.BlockSpec(memory_space=pltpu.VMEM),
+        out_shape=jax.ShapeDtypeStruct((ranks, tokens), jnp.bfloat16),
+        scratch_shapes=[
+            pltpu.VMEM(acts.shape, jnp.bfloat16),
+            pltpu.VMEM(basis.shape, jnp.bfloat16),
+            pltpu.SemaphoreType.DMA((2, PARTS)),
+        ],
+        compiler_params=pltpu.CompilerParams(vmem_limit_bytes=16 * 1024 * 1024),
+    )(acts, basis)
+
+
 def per_device(acts, out_grad, basis, first_moment, second_moment):
     splits = lax.axis_size("x")
     chips = lax.axis_size("z") * lax.axis_size("y")
     tokens = acts.shape[0]
     rank = basis.shape[1] // splits
-    local_terms = lax.dot_general(
-        basis, acts, (((0,), (1,)), ((), ())), preferred_element_type=jnp.float32
-    ).astype(jnp.bfloat16)
+    in_hbm = lambda array: pltpu.with_memory_space_constraint(array, pltpu.HBM)
+    grad_t = in_hbm(out_grad.T)
+    local_terms = project(in_hbm(acts), in_hbm(basis))
     terms = lax.all_to_all(
         local_terms.reshape(splits, rank, tokens), "x", split_axis=0, concat_axis=0, tiled=True
     )
@@ -157,7 +199,7 @@
     own = lax.all_to_all(spread, ("z", "y"), split_axis=0, concat_axis=0, tiled=True)
     other = lax.ppermute(own, "c", [(0, 1), (1, 0)])
     core = lax.axis_index("c").astype(jnp.int32).reshape(1)
-    held, partial = own_half(core, own, pltpu.with_memory_space_constraint(out_grad.T, pltpu.HBM))
+    held, partial = own_half(core, own, grad_t)
     new_first, new_second, direction = other_half_and_moments(
         core, other, held, partial, first_moment, second_moment, splits
     )

time: 96.3 us -> 95.6 us (level)
  Pallas kernels: 6.21 us -> 7.97 us
  matrix products: 2.9 us -> 1.44 us
  local copies, waits for them, and re-layouts: 1.22 us -> 0.01 us
    pallas_call x0 -> x1, Pallas kernels: none -> 1.67 us  [project(): pl.pallas_call(project_kernel, in_specs=[hbm, hbm], out_specs=pl.BlockSpe...]
    dot_general x1 -> x0, matrix products: 1.46 us -> none  [per_device(): lax.dot_general(basis, acts, (((0,), (1,)), ((), ())), preferred_element_...]
    unnamed x6, local copies, waits for them, and re-layouts: 1.22 us -> 0.01 us
where the time goes in v5:
time: 95.6 us; the launch traced here: 95.3 us
  blocking collectives  78.5 us (82%)
  Pallas kernels  7.97 us (8%)
  starting transfers between devices  6.62 us (7%)
  matrix products  1.44 us (2%)
    all_to_all x1, blocking collectives, per_device(): lax.all_to_all(spread, ('z', 'y'), split_axis=0, concat_axis=0, tiled=True)  48.7 us
    all_to_all x1, blocking collectives, per_device(): lax.all_to_all(local_terms.reshape(splits, rank, tokens), 'x', split_axis...  15 us
    all_to_all x1, blocking collectives, per_device(): lax.all_to_all(direction, 'x', split_axis=0, concat_axis=0, tiled=True)  14.8 us
    ppermute x1, starting transfers between devices, per_device(): other = lax.ppermute(own, 'c', [(0, 1), (1, 0)])  6.62 us
    pallas_call x1, Pallas kernels, own_half(): pl.pallas_call(own_kernel, in_specs=[pl.BlockSpec(memory_space=pltpu.SMEM...  3.86 us
    pallas_call x1, Pallas kernels, other_half_and_moments(): pl.pallas_call(moments_kernel, in_specs=[pl.BlockSpec(memory_space=pltpu....  2.09 us
  transfers between devices with their start and end apart: 1, of which 0 were waited for; matrix products, arithmetic and copies ran while one was open for 0% of the time, Pallas kernels for 4%

profile of v5, /device:TPU:1, one launch (start us, length us, event | category | flops | bytes accessed | tf_op | source)
XLA Modules:
  0.0 95.3 jit_solution(9965004743204045743)
XLA Ops:
  0.6 0.0 copy-start.1
  0.6 0.0 copy-start
  0.7 1.7 %shard_map.76 = bf16[512,128]{1,0:T(8,128)(2,1)S(1)} custom-call(bf16[128,1024]{1,0:T(8,128)(2,1)} %acts_ref.1, bf16[1024,512]{1,0:T(8,128)(2,1)} %basis_ref.1), custom_call_target="tpu_custom_call" | custom-call | tf_op jit(solution)/shard_map/pallas_call | solution.py:173
  2.3 15.0 %all_to_all.15.terms_ref = bf16[8,64,128]{2,1,0:T(8,128)(2,1)S(1)} all-to-all(bf16[8,64,128]{2,1,0:T(8,128)(2,1)S(1)} %bitcast.8), channel_id=1, replica_groups=mesh['x'=8,'z'=8,'y'=8,'c'=2] {'x'}, dimensions={0} | all-to-all | bytes 262144 | tf_op jit(solution)/shard_map/all_to_all | solution.py:195
  17.4 0.3 shard_map.77
  17.7 48.7 %all_to_all.16.own_ref = bf16[64,64,128]{2,1,0:T(8,128)(2,1)S(1)} all-to-all(bf16[64,64,128]{2,1,0:T(8,128)(2,1)S(1)} %shard_map.77), channel_id=1, replica_groups=mesh['x'=8,'z'=8,'y'=8,'c'=2] {'z','y'}, dimensions={0} | all-to-all | bytes 2097152 | tf_op jit(solution)/shard_map/all_to_all | solution.py:199
  66.4 6.6 %collective-permute-start = (bf16[64,64,128]{2,1,0:T(8,128)(2,1)S(1)}, bf16[64,64,128]{2,1,0:T(8,128)(2,1)S(1)}, u32[]{:S(2)}, u32[]{:S(2)}) collective-permute-start(bf16[64,64,128]{2,1,0:T(8,128)(2,1)S(1)} %all_to_all.16.own_ref), channel_id=1, source_target_pairs={{0,1},{1,0},{2,3},{3,2},{4,5},{5,4},{6,7},{7,6},{8,9},{9,8},{10,11... | collective-permute-start | bytes 3145736 | tf_op jit(solution)/shard_map/ppermute | solution.py:200
  73.1 0.0 copy-start.2
  73.1 3.9 %shard_map.78 = (bf16[224,16384]{1,0:T(8,128)(2,1)S(1)}, f32[224,64]{1,0:T(8,128)S(1)}) custom-call(s32[1]{0:T(128)} %bitcast.core_ref, bf16[64,64,128]{2,1,0:T(8,128)(2,1)S(1)} %all_to_all.16.own_ref, bf16[224,16384]{1,0:T(8,128)(2,1)} %bitcast.9), custom_call_target="tpu_custom_call" | custom-call | flops 469762048 | bytes 14680064 | tf_op jit(solution)/shard_map/pallas_call | solution.py:82
  77.0 0.0 collective-permute-done.other_ref
  77.0 0.0 copy-done.1
  77.0 0.0 copy-done
  77.0 2.1 %shard_map.79 = (f32[64,224]{1,0:T(8,128)}, f32[64,224]{1,0:T(8,128)}, bf16[8,64,224]{2,1,0:T(8,128)(2,1)S(1)}) custom-call(s32[1]{0:T(128)} %bitcast.core_ref, bf16[64,64,128]{2,1,0:T(8,128)(2,1)S(1)} %collective-permute-done.other_ref, bf16[224,16384]{1,0:T(8,128)(2,1)S(1)} %get-tuple-element.8.held_ref, f32[224,64]{1,0:T(8,128)S(1)} %get-tuple-element.9.partial_ref, ...), custom_call_target="tpu_custom_call" | custom-call | tf_op jit(solution)/shard_map/pallas_call | solution.py:127
  79.1 14.8 %all_to_all.17 = bf16[8,64,224]{2,1,0:T(8,128)(2,1)S(1)} all-to-all(bf16[8,64,224]{2,1,0:T(8,128)(2,1)S(1)} %get-tuple-element.10), channel_id=1, replica_groups=mesh['x'=8,'z'=8,'y'=8,'c'=2] {'x'}, dimensions={0} | all-to-all | bytes 458752 | tf_op jit(solution)/shard_map/all_to_all | solution.py:206
  93.9 0.0 copy-done.2
  93.9 1.4 %convolution_bitcast_fusion = f32[1024,224]{0,1:T(8,128)} fusion(bf16[512,224]{1,0:T(8,128)(2,1)S(1)} %bitcast.10, bf16[1024,512]{1,0:T(8,128)(2,1)S(1)} %copy-done.2), kind=kOutput, calls=%fused_computation | convolution fusion | flops 234881024 | bytes 2195456 | tf_op jit(solution)/shard_map/dot_general | solution.py:208
Async XLA Ops:
  0.6 76.3 %copy-start.1 = (f32[64,224]{1,0:T(8,128)S(1)}, f32[64,224]{1,0:T(8,128)}, u32[]{:S(2)}) copy-start(f32[64,224]{1,0:T(8,128)} %second_ref.1) | copy-start | bytes 172036
  0.6 76.3 %copy-start = (f32[64,224]{1,0:T(8,128)S(1)}, f32[64,224]{1,0:T(8,128)}, u32[]{:S(2)}) copy-start(f32[64,224]{1,0:T(8,128)} %first_ref.1) | copy-start | bytes 172036
  66.4 10.5 %collective-permute-start = (bf16[64,64,128]{2,1,0:T(8,128)(2,1)S(1)}, bf16[64,64,128]{2,1,0:T(8,128)(2,1)S(1)}, u32[]{:S(2)}, u32[]{:S(2)}) collective-permute-start(bf16[64,64,128]{2,1,0:T(8,128)(2,1)S(1)} %all_to_all.16.own_ref), channel_id=1, source_target_pairs={{0,1},{1,0},{2,3},{3,2},{4,5},{5,4},{6,7},{7,6},{8,9},{9,8},{10,11... | collective-permute-start | bytes 3145736 | tf_op jit(solution)/shard_map/ppermute | solution.py:200
  73.1 20.8 %copy-start.2 = (bf16[1024,512]{1,0:T(8,128)(2,1)S(1)}, bf16[1024,512]{1,0:T(8,128)(2,1)}, u32[]{:S(2)}) copy-start(bf16[1024,512]{1,0:T(8,128)(2,1)} %basis_ref.1) | copy-start | bytes 3145732

commit v6 on v4

--- a/solution.py
+++ b/solution.py
@@ -52,7 +52,7 @@
     rows = projected_ref.shape[2]
     at = lambda chip: pl.ds(pl.multiple_of((2 * chip + side) * rows, rows), rows)
     members = range(first_chip, first_chip + chips)
-    place = lambda chip: jnp.where(side == 0, chip, chip % SIDE * SIDE + chip // SIDE)
+    place = lambda chip: jnp.where(side == 1, chip, chip % SIDE * SIDE + chip // SIDE)
     projected = jnp.concatenate([projected_ref[place(chip)] for chip in members], axis=1)
     grad_t = jnp.concatenate([grad_t_ref[:, at(chip)] for chip in members], axis=1)
     return lax.dot_general(
@@ -212,9 +212,9 @@
     )
     line = lax.all_to_all(
         sum_and_spread(terms, SIDE), "fsdp", split_axis=0, concat_axis=0, tiled=True,
-        axis_index_groups=crossing(1),
-    )
-    own = exchange(line, 0).reshape(SIDE * SIDE, rank, tokens)
+        axis_index_groups=crossing(0),
+    )
+    own = exchange(line, 1).reshape(SIDE * SIDE, rank, tokens)
     other = lax.ppermute(own, "fsdp", [(at, at ^ 1) for at in range(SIDE * SIDE * CORES)])
     core = (lax.axis_index("fsdp") & (CORES - 1)).astype(jnp.int32).reshape(1)
     held, partial = own_half(core, own, grad_t)

time: 96.3 us -> 96.3 us (level)
    all_to_all x1, blocking collectives: 24 us -> 14.8 us  [per_device(): lax.all_to_all(sum_and_spread(terms, SIDE), 'fsdp', split_axis=0, concat_...]
    all_to_all x1, blocking collectives: 25 us -> 34.2 us  [exchange(): lax.all_to_all(copies, 'fsdp', split_axis=0, concat_axis=0, tiled=True, a...]
where the time goes in v6:
time: 96.3 us; the launch traced here: 96 us
  blocking collectives  78.8 us (82%)
  Pallas kernels  7.71 us (8%)
  starting transfers between devices  7.04 us (7%)
  matrix products  1.44 us (1%)
    all_to_all x1, blocking collectives, exchange(): lax.all_to_all(copies, 'fsdp', split_axis=0, concat_axis=0, tiled=True, a...  34.2 us
    all_to_all x1, blocking collectives, per_device(): lax.all_to_all(local_terms.reshape(splits, rank, tokens), 'dp', split_axi...  15 us
    all_to_all x1, blocking collectives, per_device(): lax.all_to_all(sum_and_spread(terms, SIDE), 'fsdp', split_axis=0, concat_...  14.8 us
    all_to_all x1, blocking collectives, per_device(): lax.all_to_all(direction, 'dp', split_axis=0, concat_axis=0, tiled=True)  14.8 us
    ppermute x1, starting transfers between devices, per_device(): lax.ppermute(own, 'fsdp', [(at, at ^ 1) for at in range(SIDE * SIDE * COR...  7.04 us
    pallas_call x1, Pallas kernels, own_half(): pl.pallas_call(own_kernel, in_specs=[pl.BlockSpec(memory_space=pltpu.SMEM...  3.86 us
    pallas_call x1, Pallas kernels, other_half_and_moments(): pl.pallas_call(moments_kernel, in_specs=[pl.BlockSpec(memory_space=pltpu....  2.12 us
  transfers between devices with their start and end apart: 1, of which 0 were waited for; matrix products, arithmetic and copies ran while one was open for 0% of the time, Pallas kernels for 4%

profile of v6, /device:TPU:1, one launch (start us, length us, event | category | flops | bytes accessed | tf_op | source)
XLA Modules:
  0.0 96.0 jit_solution(8773895909064301686)
XLA Ops:
  0.6 0.0 copy-start.1
  0.6 0.0 copy-start
  0.7 1.7 %shard_map.76 = bf16[512,128]{1,0:T(8,128)(2,1)S(1)} custom-call(bf16[128,1024]{1,0:T(8,128)(2,1)} %acts_ref.1, bf16[1024,512]{1,0:T(8,128)(2,1)} %basis_ref.1), custom_call_target="tpu_custom_call" | custom-call | tf_op jit(solution)/shard_map/pallas_call | solution.py:174
  2.3 15.0 %all_to_all.20.terms_ref = bf16[8,64,128]{2,1,0:T(8,128)(2,1)S(1)} all-to-all(bf16[8,64,128]{2,1,0:T(8,128)(2,1)S(1)} %bitcast.11), channel_id=1, replica_groups=mesh['dp'=8,'fsdp'=128] {'dp'}, dimensions={0} | all-to-all | bytes 262144 | tf_op jit(solution)/shard_map/all_to_all | solution.py:210
  17.4 0.1 shard_map.77
  17.4 14.8 %all_to_all.21 = bf16[8,64,128]{2,1,0:T(8,128)(2,1)S(1)} all-to-all(bf16[8,64,128]{2,1,0:T(8,128)(2,1)S(1)} %shard_map.77), channel_id=1, replica_groups={{0,16,32,48,64,80,96,112},{1,3,5,7,9,11,13,15},{2,18,34,50,66,82,98,114..., dimensions={0} | all-to-all | bytes 262144 | tf_op jit(solution)/shard_map/all_to_all | solution.py:213
  32.3 0.2 broadcast_in_dim.2
  32.5 34.2 %all_to_all.22 = bf16[8,8,64,128]{3,2,1,0:T(8,128)(2,1)S(1)} all-to-all(bf16[8,8,64,128]{3,2,1,0:T(8,128)(2,1)S(1)} %broadcast_in_dim.2), channel_id=1, replica_groups={{1,17,33,49,65,81,97,113},{0,2,4,6,8,10,12,14},{3,19,35,51,67,83,99,115..., dimensions={0} | all-to-all | bytes 2097152 | tf_op jit(solution)/shard_map/all_to_all | solution.py:198
  66.7 7.0 %collective-permute-start = (bf16[64,64,128]{2,1,0:T(8,128)(2,1)S(1)}, bf16[64,64,128]{2,1,0:T(8,128)(2,1)S(1)}, u32[]{:S(2)}, u32[]{:S(2)}) collective-permute-start(bf16[64,64,128]{2,1,0:T(8,128)(2,1)S(1)} %bitcast.9), channel_id=1, source_target_pairs={{0,1},{1,0},{2,3},{3,2},{4,5},{5,4},{6,7},{7,6},{8,9},{9,8},{10,11... | collective-permute-start | bytes 3145736 | tf_op jit(solution)/shard_map/ppermute | solution.py:218
  73.7 0.0 copy-start.2
  73.7 3.9 %shard_map.78 = (bf16[224,16384]{1,0:T(8,128)(2,1)S(1)}, f32[224,64]{1,0:T(8,128)S(1)}) custom-call(s32[1]{0:T(128)} %bitcast.core_ref, bf16[64,64,128]{2,1,0:T(8,128)(2,1)S(1)} %bitcast.10, bf16[224,16384]{1,0:T(8,128)(2,1)} %bitcast.12), custom_call_target="tpu_custom_call" | custom-call | flops 469762048 | bytes 14680064 | tf_op jit(solution)/shard_map/pallas_call | solution.py:83
  77.6 0.0 collective-permute-done.other_ref
  77.6 0.0 copy-done.1
  77.6 0.0 copy-done
  77.6 2.1 %shard_map.79 = (f32[64,224]{1,0:T(8,128)}, f32[64,224]{1,0:T(8,128)}, bf16[8,64,224]{2,1,0:T(8,128)(2,1)S(1)}) custom-call(s32[1]{0:T(128)} %bitcast.core_ref, bf16[64,64,128]{2,1,0:T(8,128)(2,1)S(1)} %collective-permute-done.other_ref, bf16[224,16384]{1,0:T(8,128)(2,1)S(1)} %get-tuple-element.8.held_ref, f32[224,64]{1,0:T(8,128)S(1)} %get-tuple-element.9.partial_ref, ...), custom_call_target="tpu_custom_call" | custom-call | tf_op jit(solution)/shard_map/pallas_call | solution.py:128
  79.8 14.8 %all_to_all.23 = bf16[8,64,224]{2,1,0:T(8,128)(2,1)S(1)} all-to-all(bf16[8,64,224]{2,1,0:T(8,128)(2,1)S(1)} %get-tuple-element.10), channel_id=1, replica_groups=mesh['dp'=8,'fsdp'=128] {'dp'}, dimensions={0} | all-to-all | bytes 458752 | tf_op jit(solution)/shard_map/all_to_all | solution.py:224
  94.6 0.0 copy-done.2
  94.6 1.4 %convolution_bitcast_fusion = f32[1024,224]{0,1:T(8,128)} fusion(bf16[512,224]{1,0:T(8,128)(2,1)S(1)} %bitcast.13, bf16[1024,512]{1,0:T(8,128)(2,1)S(1)} %copy-done.2), kind=kOutput, calls=%fused_computation | convolution fusion | flops 234881024 | bytes 2195456 | tf_op jit(solution)/shard_map/dot_general | solution.py:226
Async XLA Ops:
  0.6 77.0 %copy-start.1 = (f32[64,224]{1,0:T(8,128)S(1)}, f32[64,224]{1,0:T(8,128)}, u32[]{:S(2)}) copy-start(f32[64,224]{1,0:T(8,128)} %second_ref.1) | copy-start | bytes 172036
  0.6 77.0 %copy-start = (f32[64,224]{1,0:T(8,128)S(1)}, f32[64,224]{1,0:T(8,128)}, u32[]{:S(2)}) copy-start(f32[64,224]{1,0:T(8,128)} %first_ref.1) | copy-start | bytes 172036
  66.7 10.9 %collective-permute-start = (bf16[64,64,128]{2,1,0:T(8,128)(2,1)S(1)}, bf16[64,64,128]{2,1,0:T(8,128)(2,1)S(1)}, u32[]{:S(2)}, u32[]{:S(2)}) collective-permute-start(bf16[64,64,128]{2,1,0:T(8,128)(2,1)S(1)} %bitcast.9), channel_id=1, source_target_pairs={{0,1},{1,0},{2,3},{3,2},{4,5},{5,4},{6,7},{7,6},{8,9},{9,8},{10,11... | collective-permute-start | bytes 3145736 | tf_op jit(solution)/shard_map/ppermute | solution.py:218
  73.7 20.8 %copy-start.2 = (bf16[1024,512]{1,0:T(8,128)(2,1)S(1)}, bf16[1024,512]{1,0:T(8,128)(2,1)}, u32[]{:S(2)}) copy-start(bf16[1024,512]{1,0:T(8,128)(2,1)} %basis_ref.1) | copy-start | bytes 3145732

commit v7 on v5

--- a/solution.py
+++ b/solution.py
@@ -25,6 +25,27 @@
 
 
 CHUNKS = 8
+LANES = 128
+STRIPS = 4
+
+
+def pack(block):
+    rows, tail = block.shape[0], block.shape[1] - LANES
+    kept = rows * tail // LANES
+    step = rows - kept
+    last = [block[kept:, LANES + at : LANES + at + LANES - tail] for at in range(0, tail, LANES - tail)]
+    assert len(last) * step == kept
+    below = jnp.concatenate([block[:kept, LANES:], jnp.concatenate(last, axis=0)], axis=1)
+    return jnp.concatenate([block[:, :LANES], below], axis=0)
+
+
+def unpack(packed, rows, tail):
+    kept = packed.shape[0] - rows
+    step = rows - kept
+    beside = packed[rows:, tail:]
+    last = jnp.concatenate([beside[at : at + step] for at in range(0, kept, step)], axis=1)
+    tails = jnp.concatenate([packed[rows:, :tail], last], axis=0)
+    return jnp.concatenate([packed[:rows], tails], axis=1)
 
 
 def spread_kernel(terms_ref, spread_ref):
@@ -116,8 +137,9 @@
     new_first, new_second, direction = moments_step(total.T, first_in[...], second_in[...])
     new_first_ref[...] = new_first
     new_second_ref[...] = new_second
+    packed = pack(direction)
     for copy in range(spread_ref.shape[0]):
-        spread_ref[copy] = direction
+        spread_ref[copy] = packed
 
 
 def other_half_and_moments(core, other, held, partial, first_moment, second_moment, copies):
@@ -131,7 +153,7 @@
         out_shape=[
             jax.ShapeDtypeStruct((rank, hidden), jnp.float32),
             jax.ShapeDtypeStruct((rank, hidden), jnp.float32),
-            jax.ShapeDtypeStruct((copies, rank, hidden), jnp.bfloat16),
+            jax.ShapeDtypeStruct((copies, rank * hidden // LANES, LANES), jnp.bfloat16),
         ],
         scratch_shapes=[
             pltpu.VMEM((rank, hidden), jnp.float32),
@@ -184,6 +206,43 @@
     )(acts, basis)
 
 
+def update_kernel(pieces_ref, basis_ref, update_t_ref, strips_ref, sems):
+    hidden = update_t_ref.shape[0]
+    rank = basis_ref.shape[1] // pieces_ref.shape[0]
+    direction = jnp.concatenate(
+        [unpack(pieces_ref[split], rank, hidden - LANES) for split in range(pieces_ref.shape[0])], axis=0
+    )
+    direction_t = direction.T
+    width = basis_ref.shape[0] // STRIPS
+    writes = []
+    for strip in range(STRIPS):
+        at = pl.ds(strip * width, width)
+        strips_ref[:, at] = lax.dot_general(
+            direction_t, basis_ref[at, :], (((1,), (1,)), ((), ())), preferred_element_type=jnp.float32
+        )
+        writes.append(
+            pltpu.make_async_copy(strips_ref.at[:, at], update_t_ref.at[:, at], sems.at[strip])
+        )
+        writes[-1].start()
+    for write in writes:
+        write.wait()
+
+
+def expand(pieces, basis, hidden):
+    vmem = pl.BlockSpec(memory_space=pltpu.VMEM)
+    return pl.pallas_call(
+        update_kernel,
+        in_specs=[vmem, vmem],
+        out_specs=pl.BlockSpec(memory_space=pltpu.HBM),
+        out_shape=jax.ShapeDtypeStruct((hidden, basis.shape[0]), jnp.float32),
+        scratch_shapes=[
+            pltpu.VMEM((hidden, basis.shape[0]), jnp.float32),
+            pltpu.SemaphoreType.DMA((STRIPS,)),
+        ],
+        compiler_params=pltpu.CompilerParams(vmem_limit_bytes=24 * 1024 * 1024),
+    )(pieces, basis)
+
+
 def per_device(acts, out_grad, basis, first_moment, second_moment):
     splits = lax.axis_size("x")
     chips = lax.axis_size("z") * lax.axis_size("y")
@@ -204,8 +263,7 @@
         core, other, held, partial, first_moment, second_moment, splits
     )
     pieces = lax.all_to_all(direction, "x", split_axis=0, concat_axis=0, tiled=True)
-    piece = pieces.reshape(splits * rank, pieces.shape[2])
-    update = jnp.dot(basis, piece, preferred_element_type=jnp.float32)
+    update = expand(pieces, basis, first_moment.shape[1]).T
     return (update, new_first, new_second)
 
 

time: 95.6 us -> 95 us (level)
  Pallas kernels: 7.97 us -> 9.49 us
  matrix products: 1.44 us -> 0 us
    dot_general x1 -> x0, matrix products: 1.44 us -> none  [per_device(): update = jnp.dot(basis, piece, preferred_element_type=jnp.float32)]
    pallas_call x0 -> x1, Pallas kernels: none -> 1.41 us  [expand(): pl.pallas_call(update_kernel, in_specs=[vmem, vmem], out_specs=pl.BlockSp...]
where the time goes in v7:
time: 95 us; the launch traced here: 94.7 us
  blocking collectives  77.8 us (82%)
  Pallas kernels  9.49 us (10%)
  starting transfers between devices  6.62 us (7%)
    all_to_all x1, blocking collectives, per_device(): lax.all_to_all(spread, ('z', 'y'), split_axis=0, concat_axis=0, tiled=True)  48.7 us
    all_to_all x1, blocking collectives, per_device(): lax.all_to_all(local_terms.reshape(splits, rank, tokens), 'x', split_axis...  15 us
    all_to_all x1, blocking collectives, per_device(): lax.all_to_all(direction, 'x', split_axis=0, concat_axis=0, tiled=True)  14.1 us
    ppermute x1, starting transfers between devices, per_device(): other = lax.ppermute(own, 'c', [(0, 1), (1, 0)])  6.62 us
    pallas_call x1, Pallas kernels, own_half(): pl.pallas_call(own_kernel, in_specs=[pl.BlockSpec(memory_space=pltpu.SMEM...  3.86 us
    pallas_call x1, Pallas kernels, other_half_and_moments(): pl.pallas_call(moments_kernel, in_specs=[pl.BlockSpec(memory_space=pltpu....  2.2 us
  transfers between devices with their start and end apart: 1, of which 0 were waited for; matrix products, arithmetic and copies ran while one was open for 0% of the time, Pallas kernels for 4%

profile of v7, /device:TPU:1, one launch (start us, length us, event | category | flops | bytes accessed | tf_op | source)
XLA Modules:
  0.0 94.7 jit_solution(9367030619862019273)
XLA Ops:
  0.6 0.0 copy-start.2
  0.6 0.0 copy-start.1
  0.7 1.7 %shard_map.76 = bf16[512,128]{1,0:T(8,128)(2,1)S(1)} custom-call(bf16[128,1024]{1,0:T(8,128)(2,1)} %acts_ref.1, bf16[1024,512]{1,0:T(8,128)(2,1)} %basis_ref.3), custom_call_target="tpu_custom_call" | custom-call | tf_op jit(solution)/shard_map/pallas_call | solution.py:195
  2.3 15.0 %all_to_all.15.terms_ref = bf16[8,64,128]{2,1,0:T(8,128)(2,1)S(1)} all-to-all(bf16[8,64,128]{2,1,0:T(8,128)(2,1)S(1)} %bitcast.4), channel_id=1, replica_groups=mesh['x'=8,'z'=8,'y'=8,'c'=2] {'x'}, dimensions={0} | all-to-all | bytes 262144 | tf_op jit(solution)/shard_map/all_to_all | solution.py:254
  17.4 0.3 shard_map.77
  17.7 48.7 %all_to_all.16.own_ref = bf16[64,64,128]{2,1,0:T(8,128)(2,1)S(1)} all-to-all(bf16[64,64,128]{2,1,0:T(8,128)(2,1)S(1)} %shard_map.77), channel_id=1, replica_groups=mesh['x'=8,'z'=8,'y'=8,'c'=2] {'z','y'}, dimensions={0} | all-to-all | bytes 2097152 | tf_op jit(solution)/shard_map/all_to_all | solution.py:258
  66.4 6.6 %collective-permute-start = (bf16[64,64,128]{2,1,0:T(8,128)(2,1)S(1)}, bf16[64,64,128]{2,1,0:T(8,128)(2,1)S(1)}, u32[]{:S(2)}, u32[]{:S(2)}) collective-permute-start(bf16[64,64,128]{2,1,0:T(8,128)(2,1)S(1)} %all_to_all.16.own_ref), channel_id=1, source_target_pairs={{0,1},{1,0},{2,3},{3,2},{4,5},{5,4},{6,7},{7,6},{8,9},{9,8},{10,11... | collective-permute-start | bytes 3145736 | tf_op jit(solution)/shard_map/ppermute | solution.py:259
  73.1 0.0 copy-start
  73.1 3.9 %shard_map.78 = (bf16[224,16384]{1,0:T(8,128)(2,1)S(1)}, f32[224,64]{1,0:T(8,128)S(1)}) custom-call(s32[1]{0:T(128)} %bitcast.core_ref, bf16[64,64,128]{2,1,0:T(8,128)(2,1)S(1)} %all_to_all.16.own_ref, bf16[224,16384]{1,0:T(8,128)(2,1)} %bitcast.5), custom_call_target="tpu_custom_call" | custom-call | flops 469762048 | bytes 14680064 | tf_op jit(solution)/shard_map/pallas_call | solution.py:103
  77.0 0.0 collective-permute-done.other_ref
  77.0 0.0 copy-done.2
  77.0 0.0 copy-done.1
  77.0 2.2 %shard_map.79 = (f32[64,224]{1,0:T(8,128)}, f32[64,224]{1,0:T(8,128)}, bf16[8,112,128]{2,1,0:T(8,128)(2,1)S(1)}) custom-call(s32[1]{0:T(128)} %bitcast.core_ref, bf16[64,64,128]{2,1,0:T(8,128)(2,1)S(1)} %collective-permute-done.other_ref, bf16[224,16384]{1,0:T(8,128)(2,1)S(1)} %get-tuple-element.8.held_ref, f32[224,64]{1,0:T(8,128)S(1)} %get-tuple-element.9.partial_ref, ...), custom_call_target="tpu_custom_call" | custom-call | tf_op jit(solution)/shard_map/pallas_call | solution.py:149
  79.2 14.1 %all_to_all.17.pieces_ref = bf16[8,112,128]{2,1,0:T(8,128)(2,1)S(1)} all-to-all(bf16[8,112,128]{2,1,0:T(8,128)(2,1)S(1)} %get-tuple-element.10), channel_id=1, replica_groups=mesh['x'=8,'z'=8,'y'=8,'c'=2] {'x'}, dimensions={0} | all-to-all | bytes 458752 | tf_op jit(solution)/shard_map/all_to_all | solution.py:265
  93.3 0.0 copy-done
  93.3 1.4 %shard_map.80 = f32[224,1024]{1,0:T(8,128)} custom-call(bf16[8,112,128]{2,1,0:T(8,128)(2,1)S(1)} %all_to_all.17.pieces_ref, bf16[1024,512]{1,0:T(8,128)(2,1)S(1)} %copy-done), custom_call_target="tpu_custom_call" | custom-call | tf_op jit(solution)/shard_map/pallas_call | solution.py:233
Async XLA Ops:
  0.6 76.3 %copy-start.2 = (f32[64,224]{1,0:T(8,128)S(1)}, f32[64,224]{1,0:T(8,128)}, u32[]{:S(2)}) copy-start(f32[64,224]{1,0:T(8,128)} %second_ref.1) | copy-start | bytes 172036
  0.6 76.3 %copy-start.1 = (f32[64,224]{1,0:T(8,128)S(1)}, f32[64,224]{1,0:T(8,128)}, u32[]{:S(2)}) copy-start(f32[64,224]{1,0:T(8,128)} %first_ref.1) | copy-start | bytes 172036
  66.4 10.5 %collective-permute-start = (bf16[64,64,128]{2,1,0:T(8,128)(2,1)S(1)}, bf16[64,64,128]{2,1,0:T(8,128)(2,1)S(1)}, u32[]{:S(2)}, u32[]{:S(2)}) collective-permute-start(bf16[64,64,128]{2,1,0:T(8,128)(2,1)S(1)} %all_to_all.16.own_ref), channel_id=1, source_target_pairs={{0,1},{1,0},{2,3},{3,2},{4,5},{5,4},{6,7},{7,6},{8,9},{9,8},{10,11... | collective-permute-start | bytes 3145736 | tf_op jit(solution)/shard_map/ppermute | solution.py:259
  73.1 20.2 %copy-start = (bf16[1024,512]{1,0:T(8,128)(2,1)S(1)}, bf16[1024,512]{1,0:T(8,128)(2,1)}, u32[]{:S(2)}) copy-start(bf16[1024,512]{1,0:T(8,128)(2,1)} %basis_ref.3) | copy-start | bytes 3145732

commit v8 on v7

--- a/solution.py
+++ b/solution.py
@@ -24,7 +24,8 @@
     return (new_first, new_second, direction)
 
 
-CHUNKS = 8
+CHUNKS = 16
+PIECES = 4
 LANES = 128
 STRIPS = 4
 
@@ -128,10 +129,10 @@
     ]
     for read in reads:
         read.start()
-    chips = other_ref.shape[0] // CHUNKS
+    chips = other_ref.shape[0] // PIECES
     total = partial_ref[...]
-    for chunk in range(CHUNKS):
-        total += half_dot(1 - core_ref[0], other_ref, held_ref, chunk * chips, chips)
+    for piece in range(PIECES):
+        total += half_dot(1 - core_ref[0], other_ref, held_ref, piece * chips, chips)
     for read in reads:
         read.wait()
     new_first, new_second, direction = moments_step(total.T, first_in[...], second_in[...])

time: 95 us -> 94.9 us (level)
  no operation moved by 1% of the time
where the time goes in v8:
time: 94.9 us; the launch traced here: 94.6 us
  blocking collectives  77.8 us (82%)
  Pallas kernels  9.4 us (10%)
  starting transfers between devices  6.62 us (7%)
    all_to_all x1, blocking collectives, per_device(): lax.all_to_all(spread, ('z', 'y'), split_axis=0, concat_axis=0, tiled=True)  48.7 us
    all_to_all x1, blocking collectives, per_device(): lax.all_to_all(local_terms.reshape(splits, rank, tokens), 'x', split_axis...  15 us
    all_to_all x1, blocking collectives, per_device(): lax.all_to_all(direction, 'x', split_axis=0, concat_axis=0, tiled=True)  14.1 us
    ppermute x1, starting transfers between devices, per_device(): other = lax.ppermute(own, 'c', [(0, 1), (1, 0)])  6.62 us
    pallas_call x1, Pallas kernels, own_half(): pl.pallas_call(own_kernel, in_specs=[pl.BlockSpec(memory_space=pltpu.SMEM...  3.77 us
    pallas_call x1, Pallas kernels, other_half_and_moments(): pl.pallas_call(moments_kernel, in_specs=[pl.BlockSpec(memory_space=pltpu....  2.2 us
  transfers between devices with their start and end apart: 1, of which 0 were waited for; matrix products, arithmetic and copies ran while one was open for 0% of the time, Pallas kernels for 4%

profile of v8, /device:TPU:1, one launch (start us, length us, event | category | flops | bytes accessed | tf_op | source)
XLA Modules:
  0.0 94.6 jit_solution(7053488736187103245)
XLA Ops:
  0.6 0.0 copy-start.2
  0.6 0.0 copy-start.1
  0.7 1.7 %shard_map.76 = bf16[512,128]{1,0:T(8,128)(2,1)S(1)} custom-call(bf16[128,1024]{1,0:T(8,128)(2,1)} %acts_ref.1, bf16[1024,512]{1,0:T(8,128)(2,1)} %basis_ref.3), custom_call_target="tpu_custom_call" | custom-call | tf_op jit(solution)/shard_map/pallas_call | solution.py:196
  2.3 15.0 %all_to_all.15.terms_ref = bf16[8,64,128]{2,1,0:T(8,128)(2,1)S(1)} all-to-all(bf16[8,64,128]{2,1,0:T(8,128)(2,1)S(1)} %bitcast.4), channel_id=1, replica_groups=mesh['x'=8,'z'=8,'y'=8,'c'=2] {'x'}, dimensions={0} | all-to-all | bytes 262144 | tf_op jit(solution)/shard_map/all_to_all | solution.py:255
  17.4 0.3 shard_map.77
  17.7 48.7 %all_to_all.16.own_ref = bf16[64,64,128]{2,1,0:T(8,128)(2,1)S(1)} all-to-all(bf16[64,64,128]{2,1,0:T(8,128)(2,1)S(1)} %shard_map.77), channel_id=1, replica_groups=mesh['x'=8,'z'=8,'y'=8,'c'=2] {'z','y'}, dimensions={0} | all-to-all | bytes 2097152 | tf_op jit(solution)/shard_map/all_to_all | solution.py:259
  66.4 6.6 %collective-permute-start = (bf16[64,64,128]{2,1,0:T(8,128)(2,1)S(1)}, bf16[64,64,128]{2,1,0:T(8,128)(2,1)S(1)}, u32[]{:S(2)}, u32[]{:S(2)}) collective-permute-start(bf16[64,64,128]{2,1,0:T(8,128)(2,1)S(1)} %all_to_all.16.own_ref), channel_id=1, source_target_pairs={{0,1},{1,0},{2,3},{3,2},{4,5},{5,4},{6,7},{7,6},{8,9},{9,8},{10,11... | collective-permute-start | bytes 3145736 | tf_op jit(solution)/shard_map/ppermute | solution.py:260
  73.1 0.0 copy-start
  73.1 3.8 %shard_map.78 = (bf16[224,16384]{1,0:T(8,128)(2,1)S(1)}, f32[224,64]{1,0:T(8,128)S(1)}) custom-call(s32[1]{0:T(128)} %bitcast.core_ref, bf16[64,64,128]{2,1,0:T(8,128)(2,1)S(1)} %all_to_all.16.own_ref, bf16[224,16384]{1,0:T(8,128)(2,1)} %bitcast.5), custom_call_target="tpu_custom_call" | custom-call | flops 469762048 | bytes 14680064 | tf_op jit(solution)/shard_map/pallas_call | solution.py:104
  76.9 0.0 collective-permute-done.other_ref
  76.9 0.0 copy-done.2
  76.9 0.0 copy-done.1
  76.9 2.2 %shard_map.79 = (f32[64,224]{1,0:T(8,128)}, f32[64,224]{1,0:T(8,128)}, bf16[8,112,128]{2,1,0:T(8,128)(2,1)S(1)}) custom-call(s32[1]{0:T(128)} %bitcast.core_ref, bf16[64,64,128]{2,1,0:T(8,128)(2,1)S(1)} %collective-permute-done.other_ref, bf16[224,16384]{1,0:T(8,128)(2,1)S(1)} %get-tuple-element.8.held_ref, f32[224,64]{1,0:T(8,128)S(1)} %get-tuple-element.9.partial_ref, ...), custom_call_target="tpu_custom_call" | custom-call | tf_op jit(solution)/shard_map/pallas_call | solution.py:150
  79.1 14.1 %all_to_all.17.pieces_ref = bf16[8,112,128]{2,1,0:T(8,128)(2,1)S(1)} all-to-all(bf16[8,112,128]{2,1,0:T(8,128)(2,1)S(1)} %get-tuple-element.10), channel_id=1, replica_groups=mesh['x'=8,'z'=8,'y'=8,'c'=2] {'x'}, dimensions={0} | all-to-all | bytes 458752 | tf_op jit(solution)/shard_map/all_to_all | solution.py:266
  93.2 0.0 copy-done
  93.2 1.4 %shard_map.80 = f32[224,1024]{1,0:T(8,128)} custom-call(bf16[8,112,128]{2,1,0:T(8,128)(2,1)S(1)} %all_to_all.17.pieces_ref, bf16[1024,512]{1,0:T(8,128)(2,1)S(1)} %copy-done), custom_call_target="tpu_custom_call" | custom-call | tf_op jit(solution)/shard_map/pallas_call | solution.py:234
Async XLA Ops:
  0.6 76.2 %copy-start.2 = (f32[64,224]{1,0:T(8,128)S(1)}, f32[64,224]{1,0:T(8,128)}, u32[]{:S(2)}) copy-start(f32[64,224]{1,0:T(8,128)} %second_ref.1) | copy-start | bytes 172036
  0.6 76.2 %copy-start.1 = (f32[64,224]{1,0:T(8,128)S(1)}, f32[64,224]{1,0:T(8,128)}, u32[]{:S(2)}) copy-start(f32[64,224]{1,0:T(8,128)} %first_ref.1) | copy-start | bytes 172036
  66.4 10.4 %collective-permute-start = (bf16[64,64,128]{2,1,0:T(8,128)(2,1)S(1)}, bf16[64,64,128]{2,1,0:T(8,128)(2,1)S(1)}, u32[]{:S(2)}, u32[]{:S(2)}) collective-permute-start(bf16[64,64,128]{2,1,0:T(8,128)(2,1)S(1)} %all_to_all.16.own_ref), channel_id=1, source_target_pairs={{0,1},{1,0},{2,3},{3,2},{4,5},{5,4},{6,7},{7,6},{8,9},{9,8},{10,11... | collective-permute-start | bytes 3145736 | tf_op jit(solution)/shard_map/ppermute | solution.py:260
  73.1 20.1 %copy-start = (bf16[1024,512]{1,0:T(8,128)(2,1)S(1)}, bf16[1024,512]{1,0:T(8,128)(2,1)}, u32[]{:S(2)}) copy-start(bf16[1024,512]{1,0:T(8,128)(2,1)} %basis_ref.3) | copy-start | bytes 3145732

commit v9 on v8

--- a/solution.py
+++ b/solution.py
@@ -207,7 +207,14 @@
     )(acts, basis)
 
 
-def update_kernel(pieces_ref, basis_ref, update_t_ref, strips_ref, sems):
+def update_kernel(pieces_ref, basis_ref, first_ref, second_ref,
+                  update_t_ref, new_first_ref, new_second_ref, strips_ref, sems):
+    writes = [
+        pltpu.make_async_copy(first_ref, new_first_ref, sems.at[STRIPS]),
+        pltpu.make_async_copy(second_ref, new_second_ref, sems.at[STRIPS + 1]),
+    ]
+    for write in writes:
+        write.start()
     hidden = update_t_ref.shape[0]
     rank = basis_ref.shape[1] // pieces_ref.shape[0]
     direction = jnp.concatenate(
@@ -215,7 +222,6 @@
     )
     direction_t = direction.T
     width = basis_ref.shape[0] // STRIPS
-    writes = []
     for strip in range(STRIPS):
         at = pl.ds(strip * width, width)
         strips_ref[:, at] = lax.dot_general(
@@ -229,19 +235,24 @@
         write.wait()
 
 
-def expand(pieces, basis, hidden):
+def expand(pieces, basis, new_first, new_second):
+    hidden = new_first.shape[1]
     vmem = pl.BlockSpec(memory_space=pltpu.VMEM)
     return pl.pallas_call(
         update_kernel,
-        in_specs=[vmem, vmem],
-        out_specs=pl.BlockSpec(memory_space=pltpu.HBM),
-        out_shape=jax.ShapeDtypeStruct((hidden, basis.shape[0]), jnp.float32),
+        in_specs=[vmem, vmem, vmem, vmem],
+        out_specs=[pl.BlockSpec(memory_space=pltpu.HBM)] * 3,
+        out_shape=[
+            jax.ShapeDtypeStruct((hidden, basis.shape[0]), jnp.float32),
+            jax.ShapeDtypeStruct(new_first.shape, jnp.float32),
+            jax.ShapeDtypeStruct(new_second.shape, jnp.float32),
+        ],
         scratch_shapes=[
             pltpu.VMEM((hidden, basis.shape[0]), jnp.float32),
-            pltpu.SemaphoreType.DMA((STRIPS,)),
+            pltpu.SemaphoreType.DMA((STRIPS + 2,)),
         ],
         compiler_params=pltpu.CompilerParams(vmem_limit_bytes=24 * 1024 * 1024),
-    )(pieces, basis)
+    )(pieces, basis, new_first, new_second)
 
 
 def per_device(acts, out_grad, basis, first_moment, second_moment):
@@ -264,8 +275,8 @@
         core, other, held, partial, first_moment, second_moment, splits
     )
     pieces = lax.all_to_all(direction, "x", split_axis=0, concat_axis=0, tiled=True)
-    update = expand(pieces, basis, first_moment.shape[1]).T
-    return (update, new_first, new_second)
+    update_t, new_first, new_second = expand(pieces, basis, new_first, new_second)
+    return (update_t.T, new_first, new_second)
 
 
 def solution(mesh):

time: 94.9 us -> 94.3 us (level)
  no operation moved by 1% of the time
where the time goes in v9:
time: 94.3 us; the launch traced here: 94 us
  blocking collectives  77.8 us (83%)
  Pallas kernels  8.81 us (9%)
  starting transfers between devices  6.62 us (7%)
    all_to_all x1, blocking collectives, per_device(): lax.all_to_all(spread, ('z', 'y'), split_axis=0, concat_axis=0, tiled=True)  48.7 us
    all_to_all x1, blocking collectives, per_device(): lax.all_to_all(local_terms.reshape(splits, rank, tokens), 'x', split_axis...  15 us
    all_to_all x1, blocking collectives, per_device(): lax.all_to_all(direction, 'x', split_axis=0, concat_axis=0, tiled=True)  14.1 us
    ppermute x1, starting transfers between devices, per_device(): other = lax.ppermute(own, 'c', [(0, 1), (1, 0)])  6.62 us
    pallas_call x1, Pallas kernels, own_half(): pl.pallas_call(own_kernel, in_specs=[pl.BlockSpec(memory_space=pltpu.SMEM...  3.77 us
  transfers between devices with their start and end apart: 1, of which 0 were waited for; matrix products, arithmetic and copies ran while one was open for 0% of the time, Pallas kernels for 4%

profile of v9, /device:TPU:1, one launch (start us, length us, event | category | flops | bytes accessed | tf_op | source)
XLA Modules:
  0.0 94.0 jit_solution(11945694058108278200)
XLA Ops:
  0.6 0.0 copy-start.2
  0.6 0.0 copy-start.1
  0.7 1.7 %shard_map.76 = bf16[512,128]{1,0:T(8,128)(2,1)S(1)} custom-call(bf16[128,1024]{1,0:T(8,128)(2,1)} %acts_ref.1, bf16[1024,512]{1,0:T(8,128)(2,1)} %basis_ref.3), custom_call_target="tpu_custom_call" | custom-call | tf_op jit(solution)/shard_map/pallas_call | solution.py:196
  2.3 15.0 %all_to_all.15.terms_ref = bf16[8,64,128]{2,1,0:T(8,128)(2,1)S(1)} all-to-all(bf16[8,64,128]{2,1,0:T(8,128)(2,1)S(1)} %bitcast.4), channel_id=1, replica_groups=mesh['x'=8,'z'=8,'y'=8,'c'=2] {'x'}, dimensions={0} | all-to-all | bytes 262144 | tf_op jit(solution)/shard_map/all_to_all | solution.py:266
  17.4 0.3 shard_map.77
  17.7 48.7 %all_to_all.16.own_ref = bf16[64,64,128]{2,1,0:T(8,128)(2,1)S(1)} all-to-all(bf16[64,64,128]{2,1,0:T(8,128)(2,1)S(1)} %shard_map.77), channel_id=1, replica_groups=mesh['x'=8,'z'=8,'y'=8,'c'=2] {'z','y'}, dimensions={0} | all-to-all | bytes 2097152 | tf_op jit(solution)/shard_map/all_to_all | solution.py:270
  66.4 6.6 %collective-permute-start = (bf16[64,64,128]{2,1,0:T(8,128)(2,1)S(1)}, bf16[64,64,128]{2,1,0:T(8,128)(2,1)S(1)}, u32[]{:S(2)}, u32[]{:S(2)}) collective-permute-start(bf16[64,64,128]{2,1,0:T(8,128)(2,1)S(1)} %all_to_all.16.own_ref), channel_id=1, source_target_pairs={{0,1},{1,0},{2,3},{3,2},{4,5},{5,4},{6,7},{7,6},{8,9},{9,8},{10,11... | collective-permute-start | bytes 3145736 | tf_op jit(solution)/shard_map/ppermute | solution.py:271
  73.1 0.0 copy-start
  73.1 3.8 %shard_map.78 = (bf16[224,16384]{1,0:T(8,128)(2,1)S(1)}, f32[224,64]{1,0:T(8,128)S(1)}) custom-call(s32[1]{0:T(128)} %bitcast.core_ref, bf16[64,64,128]{2,1,0:T(8,128)(2,1)S(1)} %all_to_all.16.own_ref, bf16[224,16384]{1,0:T(8,128)(2,1)} %bitcast.5), custom_call_target="tpu_custom_call" | custom-call | flops 469762048 | bytes 14680064 | tf_op jit(solution)/shard_map/pallas_call | solution.py:104
  76.9 0.0 collective-permute-done.other_ref
  76.9 0.0 copy-done.2
  76.9 0.0 copy-done.1
  76.9 1.6 %shard_map.79 = (f32[64,224]{1,0:T(8,128)S(1)}, f32[64,224]{1,0:T(8,128)S(1)}, bf16[8,112,128]{2,1,0:T(8,128)(2,1)S(1)}) custom-call(s32[1]{0:T(128)} %bitcast.core_ref, bf16[64,64,128]{2,1,0:T(8,128)(2,1)S(1)} %collective-permute-done.other_ref, bf16[224,16384]{1,0:T(8,128)(2,1)S(1)} %get-tuple-element.11.held_ref, ...), custom_call_target="tpu_custom_call" | custom-call | tf_op jit(solution)/shard_map/pallas_call | solution.py:150
  78.5 14.1 %all_to_all.17.pieces_ref = bf16[8,112,128]{2,1,0:T(8,128)(2,1)S(1)} all-to-all(bf16[8,112,128]{2,1,0:T(8,128)(2,1)S(1)} %get-tuple-element.13), channel_id=1, replica_groups=mesh['x'=8,'z'=8,'y'=8,'c'=2] {'x'}, dimensions={0} | all-to-all | bytes 458752 | tf_op jit(solution)/shard_map/all_to_all | solution.py:277
  92.6 0.0 copy-done
  92.6 1.4 %shard_map.80 = (f32[224,1024]{1,0:T(8,128)}, f32[64,224]{1,0:T(8,128)}, f32[64,224]{1,0:T(8,128)}) custom-call(bf16[8,112,128]{2,1,0:T(8,128)(2,1)S(1)} %all_to_all.17.pieces_ref, bf16[1024,512]{1,0:T(8,128)(2,1)S(1)} %copy-done, f32[64,224]{1,0:T(8,128)S(1)} %get-tuple-element.14.first_ref, f32[64,224]{1,0:T(8,128)S(1)} %get-tuple-element.15.second_ref), custom_call_target="tpu_custom_call" | custom-call | tf_op jit(solution)/shard_map/pallas_call | solution.py:241
Async XLA Ops:
  0.6 76.2 %copy-start.2 = (f32[64,224]{1,0:T(8,128)S(1)}, f32[64,224]{1,0:T(8,128)}, u32[]{:S(2)}) copy-start(f32[64,224]{1,0:T(8,128)} %second_ref.1) | copy-start | bytes 172036
  0.6 76.2 %copy-start.1 = (f32[64,224]{1,0:T(8,128)S(1)}, f32[64,224]{1,0:T(8,128)}, u32[]{:S(2)}) copy-start(f32[64,224]{1,0:T(8,128)} %first_ref.1) | copy-start | bytes 172036
  66.4 10.4 %collective-permute-start = (bf16[64,64,128]{2,1,0:T(8,128)(2,1)S(1)}, bf16[64,64,128]{2,1,0:T(8,128)(2,1)S(1)}, u32[]{:S(2)}, u32[]{:S(2)}) collective-permute-start(bf16[64,64,128]{2,1,0:T(8,128)(2,1)S(1)} %all_to_all.16.own_ref), channel_id=1, source_target_pairs={{0,1},{1,0},{2,3},{3,2},{4,5},{5,4},{6,7},{7,6},{8,9},{9,8},{10,11... | collective-permute-start | bytes 3145736 | tf_op jit(solution)/shard_map/ppermute | solution.py:271
  73.1 19.5 %copy-start = (bf16[1024,512]{1,0:T(8,128)(2,1)S(1)}, bf16[1024,512]{1,0:T(8,128)(2,1)}, u32[]{:S(2)}) copy-start(bf16[1024,512]{1,0:T(8,128)(2,1)} %basis_ref.3) | copy-start | bytes 3145732
